TPU v7x, 32 devices: a whole 2x2x4 slice. The times are simulated.
32 devices in a mesh: gx: 4 (over y, core), gy: 8 (over z, x).
Axes of the slice: x: 2, y: 2, z: 4, core: 2. Of those that a mesh axis runs over, the one named last changes fastest.
Arguments:
- rhs: float32 [32, 64, 512], P('gx', 'gy'), may hold values from -18 to 18
- diag: float32 [32, 64, 512], P('gx', 'gy'), may hold values from 0.5 to 2
- smoother_center: float32 [32, 64, 512], P('gx', 'gy'), may hold values from 0.1 to 0.2
- smoother_faces: float32 [6, 32, 64, 512], P(None, 'gx', 'gy'), may hold values from 0.01 to 0.05
- send_count: int32 [4, 8, 8], P('gx', 'gy'), may hold values from 0 to 4096, as said below
- send_cell: int32 [4, 8, 8, 4096], P('gx', 'gy'), may hold values from 0 to 32767, as said below
- restrict_col: int32 [27, 4, 8, 4096], P(None, 'gx', 'gy'), may hold values from 0 to 65535, as said below
- restrict_vals: float32 [27, 4, 8, 4096], P(None, 'gx', 'gy'), may hold values from 0.03 to 0.2
- coarse_col: int32 [16, 4, 8, 4096], P(None, 'gx', 'gy'), may hold values from 0 to 12287, as said below
- coarse_diag: float32 [4, 8, 4096], P('gx', 'gy'), may hold values from 3 to 6
- coarse_vals: float32 [16, 4, 8, 4096], P(None, 'gx', 'gy'), may hold values from -3 to 3
- csmooth_diag: float32 [4, 8, 4096], P('gx', 'gy'), may hold values from 0.15 to 0.3
- csmooth_vals: float32 [16, 4, 8, 4096], P(None, 'gx', 'gy'), may hold values from -0.3 to 0.3
- remote_row: int32 [4, 4, 8, 8, 4096], P(None, 'gx', 'gy'), may hold values from 0 to 4095, as said below
- remote_vals: float32 [4, 4, 8, 8, 4096], P(None, 'gx', 'gy'), may hold values from 0.3 to 1
- interp_row: int32 [4, 32, 64, 512], P(None, 'gx', 'gy'), may hold values from 0 to 4095, as said below
- interp_vals: float32 [4, 32, 64, 512], P(None, 'gx', 'gy'), may hold values from 0.3 to 1
Outputs:
- solution: float32 [32, 64, 512], P('gx', 'gy')
- residual: float32 [32, 64, 512], P('gx', 'gy')
Inputs may be any that keep to these rules, and one draw needn't show every extreme that they name: `send_count`: zero towards a neighbour outside the grid; one device receives 4096 used slots from each of its eight neighbours, and about a quarter of the devices receive several times more than the rest. `send_cell`: the cell of a slot towards direction d lies within 2 cells of the side facing that neighbour, within 4 cells of both sides for a diagonal neighbour. The slots of one direction in one aligned block of 128 slots lie in one run of 128 cells along z that starts at a multiple of 128. `restrict_col`: only a device's first 1024 coarse rows read received slots. For one k, the entries of one aligned block of 128 coarse rows lie in one aligned block of 128 columns. `coarse_col`: only a device's first 1024 coarse rows read neighbours' rows. For one k, the entries of one aligned block of 128 coarse rows lie in one aligned block of 128 columns. `remote_row`: for one k and one direction, the entries of one aligned block of 128 slots lie in one aligned block of 128 coarse rows. `interp_row`: for one k, the entries of one run of 128 cells along z that starts at a multiple of 128 lie in one aligned block of 128 coarse rows.
All inputs are finite; a program needn't handle non-finite values.
Results may differ from a plain program's by a relative error of at most 0.0003.
Values sent between devices are 32-bit elements; how exact they have to be, the bound alone decides.
A program may use at most 128 MiB of HBM per device.

v0:
```python
import jax
import jax.numpy as jnp
from jax import lax
from jax.experimental import pallas as pl
from jax.experimental.pallas import tpu as pltpu
from jax.sharding import PartitionSpec as P

BLK = 128
OFFSETS = ((-1, -1), (-1, 0), (-1, 1), (0, -1), (0, 1), (1, -1), (1, 0), (1, 1))
SIDES = ((-1, 0), (1, 0), (0, -1), (0, 1))
MESH_ID = pl.DeviceIdType.MESH


def split_two(table):
    high = table.astype(jnp.bfloat16)
    low = (table - high.astype(jnp.float32)).astype(jnp.bfloat16)
    return jnp.concatenate([high, low], axis=1)


def one_hot(base, width):
    ids = lax.broadcasted_iota(jnp.int32, (base.shape[0], width), 1)
    return jnp.where(ids == base, 1.0, 0.0).astype(jnp.bfloat16)


def pick(index, base, table_two):
    both = jnp.dot(
        one_hot(base, table_two.shape[0]), table_two, preferred_element_type=jnp.float32
    )
    rows = both[:, :BLK] + both[:, BLK:]
    return jnp.take_along_axis(rows, index & (BLK - 1), axis=1, mode="promise_in_bounds")


def make_kernel(sizes, shapes):
    na, nb = sizes
    cx, cy, nz = shapes["rhs"]
    zblocks = nz // BLK
    cells = cx * cy
    fine_rows = cells * zblocks
    cap = shapes["send_cell"][1]
    slots = cap // BLK
    kr, crows, _ = shapes["restrict_col"]
    ka = shapes["coarse_col"][0]
    ki = shapes["interp_row"][0]
    rim_rows = 8

    def fine_place(block):
        return (block % zblocks) * cells + block // zblocks

    def kernel(
        rhs_h, diag_h, center_h, faces_h, count_ref, cell_h, rcol_h, rval_h, ccol_h,
        cdiag_h, cval_h, mdiag_h, mval_h, rrow_h, rrval_h, irow_h, ival_h,
        sol_ref, res_ref,
        field, ysend, yrecv, diag, center, faces, cell, rcol, rval, ccol, cdiag, cval,
        mdiag, mval, rrow, rrval, irow, ival, resid, fine_two, choose, sent, received,
        back, returned, coarse, rim, spread, partial,
        in_sem, halo_send, halo_recv, slot_send, slot_recv, back_send, back_recv,
        rim_send, rim_recv,
    ):
        a = lax.axis_index("gx")
        b = lax.axis_index("gy")

        loads = [
            (rhs_h, field.at[0, pl.ds(1, cx)]), (center_h, center), (faces_h, faces),
            (diag_h, diag), (cell_h, cell), (rcol_h, rcol), (rval_h, rval),
            (ccol_h, ccol), (mdiag_h, mdiag), (mval_h, mval), (cdiag_h, cdiag),
            (cval_h, cval), (rrow_h, rrow), (rrval_h, rrval), (irow_h, irow),
            (ival_h, ival),
        ]
        loads = [
            pltpu.make_async_copy(source, target, in_sem.at[n])
            for n, (source, target) in enumerate(loads)
        ]
        for load in loads:
            load.start()

        def there(step):
            dx, dy = step
            checks = []
            if dx < 0:
                checks.append(a > 0)
            if dx > 0:
                checks.append(a < na - 1)
            if dy < 0:
                checks.append(b > 0)
            if dy > 0:
                checks.append(b < nb - 1)
            out = checks[0]
            for check in checks[1:]:
                out = jnp.logical_and(out, check)
            return out

        exists = [there(step) for step in OFFSETS]
        side_exists = [there(step) for step in SIDES]

        barrier = pltpu.get_barrier_semaphore()
        total = jnp.int32(0)
        for d, (dx, dy) in enumerate(OFFSETS):
            @pl.when(exists[d])
            def _():
                pl.semaphore_signal(
                    barrier, inc=1, device_id=(a + dx, b + dy), device_id_type=MESH_ID
                )
            total = total + exists[d].astype(jnp.int32)

        for s in range(4):
            @pl.when(jnp.logical_not(side_exists[s]))
            def _():
                for t in range(5):
                    if s < 2:
                        field[t, 0 if s == 0 else cx + 1] = jnp.zeros((cy, nz), jnp.float32)
                    else:
                        yrecv[t, s - 2] = jnp.zeros((cx, nz), jnp.float32)
        for d in range(8):
            @pl.when(jnp.logical_not(exists[d]))
            def _():
                received[d] = jnp.zeros((slots, BLK), jnp.float32)
                returned[d] = jnp.zeros((slots, BLK), jnp.float32)
                for t in range(3):
                    rim[t, d] = jnp.zeros((rim_rows, BLK), jnp.float32)

        def halo_copy(t, s):
            dx, dy = SIDES[s]
            if s == 0:
                src, dst = field.at[t, 1], field.at[t, cx + 1]
            elif s == 1:
                src, dst = field.at[t, cx], field.at[t, 0]
            else:
                src, dst = ysend.at[t, s - 2], yrecv.at[t, 3 - s]
            return pltpu.make_async_remote_copy(
                src_ref=src, dst_ref=dst, send_sem=halo_send.at[t, s],
                recv_sem=halo_recv.at[t, s ^ 1],
                device_id=(a + dx, b + dy), device_id_type=MESH_ID,
            )

        def halo_arrival(t, s):
            dx, dy = SIDES[s]
            dst = field.at[t, 0 if s == 0 else cx + 1] if s < 2 else yrecv.at[t, s - 2]
            return pltpu.make_async_remote_copy(
                src_ref=dst, dst_ref=dst, send_sem=halo_send.at[t, s],
                recv_sem=halo_recv.at[t, s],
                device_id=(a + dx, b + dy), device_id_type=MESH_ID,
            )

        def start_halo(t):
            for s in (2, 3, 0, 1):
                @pl.when(side_exists[s])
                def _():
                    halo_copy(t, s).start()

        def wait_halo(t):
            for s in range(4):
                @pl.when(side_exists[s])
                def _():
                    halo_arrival(t, s).wait_recv()

        def eight_copy(src, dst, send_sem, recv_sem, d):
            dx, dy = OFFSETS[d]
            return pltpu.make_async_remote_copy(
                src_ref=src(d), dst_ref=dst(7 - d), send_sem=send_sem(d),
                recv_sem=recv_sem(7 - d),
                device_id=(a + dx, b + dy), device_id_type=MESH_ID,
            )

        def eight_arrival(dst, send_sem, recv_sem, d):
            dx, dy = OFFSETS[d]
            return pltpu.make_async_remote_copy(
                src_ref=dst(d), dst_ref=dst(d), send_sem=send_sem(d), recv_sem=recv_sem(d),
                device_id=(a + dx, b + dy), device_id_type=MESH_ID,
            )

        slot_plan = (
            lambda d: sent.at[d], lambda d: received.at[d],
            lambda d: slot_send.at[d], lambda d: slot_recv.at[d],
        )
        back_plan = (
            lambda d: back.at[d], lambda d: returned.at[d],
            lambda d: back_send.at[d], lambda d: back_recv.at[d],
        )

        def rim_plan(t):
            return (
                lambda d: coarse.at[t, pl.ds(0, rim_rows)], lambda d: rim.at[t, d],
                lambda d: rim_send.at[t, d], lambda d: rim_recv.at[t, d],
            )

        def start_eight(plan):
            for d in (0, 2, 5, 7, 3, 4, 1, 6):
                @pl.when(exists[d])
                def _():
                    eight_copy(*plan, d).start()

        def wait_eight(plan):
            for d in range(8):
                @pl.when(exists[d])
                def _():
                    eight_arrival(*plan[1:], d).wait_recv()

        row_ids = lax.broadcasted_iota(jnp.int32, (cy, nz), 0)
        lane_ids = lax.broadcasted_iota(jnp.int32, (cy, nz), 1)

        zeros = jnp.zeros((cy, nz), jnp.float32)

        def beside(t, i):
            centre = field[t, i + 1]
            return centre, [
                field[t, i] if i > 0 else zeros,
                field[t, i + 2] if i < cx - 1 else zeros,
                jnp.where(row_ids == 0, 0.0, pltpu.roll(centre, 1, 0)),
                jnp.where(row_ids == cy - 1, 0.0, pltpu.roll(centre, cy - 1, 0)),
                jnp.where(lane_ids == 0, 0.0, pltpu.roll(centre, 1, 1)),
                jnp.where(lane_ids == nz - 1, 0.0, pltpu.roll(centre, nz - 1, 1)),
            ]

        def sides(t, i):
            out = [
                jnp.where(row_ids == 0, jnp.broadcast_to(yrecv[t, 0, i:i + 1, :], (cy, nz)), 0.0),
                jnp.where(row_ids == cy - 1, jnp.broadcast_to(yrecv[t, 1, i:i + 1, :], (cy, nz)), 0.0),
            ]
            return [
                field[t, 0] if i == 0 else None,
                field[t, cx + 1] if i == cx - 1 else None,
            ] + out

        def residual_inside(t):
            for i in range(cx):
                centre, near = beside(t, i)
                sums = near[0]
                for one in near[1:]:
                    sums = sums + one
                partial[i] = field[0, i + 1] - ((6.0 + diag[i]) * centre - sums)

        def residual_row(t, i):
            out = partial[i]
            for one in sides(t, i):
                if one is not None:
                    out = out + one
            return out

        def smoother_inside(t, base):
            for i in range(cx):
                centre, near = beside(t, i)
                out = center[i] * centre
                for q in range(6):
                    out = out + faces[q, i] * near[q]
                partial[i] = out if base is None else field[base, i + 1] + out

        def smoother_row(t, i):
            out = partial[i]
            for q, one in enumerate(sides(t, i)):
                if one is not None:
                    out = out + faces[q, i] * one
            return out

        def put(t, i, value):
            field[t, i + 1] = value
            ysend[t, 0, i:i + 1, :] = value[0:1]
            ysend[t, 1, i:i + 1, :] = value[cy - 1:cy]

        loads[0].wait()
        for i in range(cx):
            value = field[0, i + 1]
            ysend[0, 0, i:i + 1, :] = value[0:1]
            ysend[0, 1, i:i + 1, :] = value[cy - 1:cy]
        pl.semaphore_wait(barrier, total)
        start_halo(0)
        for load in loads[1:5]:
            load.wait()

        cell_index = jnp.concatenate(
            [cell[:, s * BLK:(s + 1) * BLK] for s in range(slots)], axis=0
        )
        cell_base = fine_place(cell_index[:, 0:1] // BLK)
        across = jnp.transpose(
            jnp.broadcast_to(cell_base, (8 * slots, BLK)).astype(jnp.float32)
        )[0:1].astype(jnp.int32)
        fine_ids = lax.broadcasted_iota(jnp.int32, (fine_rows, 8 * slots), 0)
        choose[...] = jnp.where(fine_ids == across, 1.0, 0.0).astype(jnp.bfloat16)

        smoother_inside(0, None)
        wait_halo(0)
        for i in range(cx):
            put(1, i, smoother_row(0, i))
        start_halo(1)
        residual_inside(1)
        for load in loads[5:]:
            load.wait()

        wait_halo(1)
        for i in range(cx):
            resid[i] = residual_row(1, i)
        table = jnp.concatenate(
            [resid[:, :, z * BLK:(z + 1) * BLK].reshape(cells, BLK) for z in range(zblocks)],
            axis=0,
        )
        fine_two[...] = split_two(table)

        picked = pick(cell_index, cell_base, fine_two[...])
        lanes = lax.broadcasted_iota(jnp.int32, (8, BLK), 1)
        for s in range(slots):
            live = lanes + s * BLK < count_ref[...]
            values = jnp.where(live, picked[8 * s:8 * s + 8], 0.0)
            for d in range(8):
                sent[d, s:s + 1, :] = values[d:d + 1]
        start_eight(slot_plan)

        step = 9 if kr % 9 == 0 else 1

        def restrict_some(c, acc):
            index = rcol[pl.ds(c * step, step)].reshape(step * crows, BLK)
            block = index[:, 0:1] // BLK
            base = jnp.where(block < fine_rows, fine_place(block), -1)
            got = pick(index, base, fine_two[...]).reshape(step, crows, BLK)
            return acc + jnp.sum(got * rval[pl.ds(c * step, step)], axis=0)

        rc = lax.fori_loop(
            0, kr // step, restrict_some, jnp.zeros((crows, BLK), jnp.float32)
        )
        wait_eight(slot_plan)
        received_two = split_two(received[...].reshape(8 * slots, BLK))
        index = rcol[:, 0:rim_rows, :].reshape(kr * rim_rows, BLK)
        got = pick(index, index[:, 0:1] // BLK - fine_rows, received_two)
        more = jnp.sum(
            got.reshape(kr, rim_rows, BLK) * rval[:, 0:rim_rows, :], axis=0
        )
        rc = jnp.concatenate([rc[:rim_rows] + more, rc[rim_rows:]], axis=0)

        def coarse_apply(t, vector, diagonal, values):
            coarse[t] = vector
            start_eight(rim_plan(t))
            index = ccol[...].reshape(ka * crows, BLK)
            got = pick(index, index[:, 0:1] // BLK, split_two(vector))
            own = diagonal[...] * vector + jnp.sum(
                got.reshape(ka, crows, BLK) * values[...], axis=0
            )
            wait_eight(rim_plan(t))
            index = ccol[:, 0:rim_rows, :].reshape(ka * rim_rows, BLK)
            got = pick(
                index, index[:, 0:1] // BLK - crows,
                split_two(rim[t].reshape(8 * rim_rows, BLK)),
            )
            more = jnp.sum(
                got.reshape(ka, rim_rows, BLK) * values[:, 0:rim_rows, :], axis=0
            )
            return jnp.concatenate([own[:rim_rows] + more, own[rim_rows:]], axis=0)

        xc1 = coarse_apply(0, rc, mdiag, mval)
        rc2 = rc - coarse_apply(1, xc1, cdiag, cval)
        xc2 = xc1 + coarse_apply(2, rc2, mdiag, mval)
        coarse_two = split_two(xc2)

        group = 8 if slots % 8 == 0 else 1
        for c in range(slots // group):
            parts = [(c * group + g) * BLK for g in range(group)]
            index = jnp.concatenate(
                [rrow[:, :, p:p + BLK].reshape(ki * 8, BLK) for p in parts], axis=0
            )
            got = pick(index, index[:, 0:1] // BLK, coarse_two)
            for g, p in enumerate(parts):
                mine = got[g * ki * 8:(g + 1) * ki * 8].reshape(ki, 8, BLK)
                values = jnp.sum(mine * rrval[:, :, p:p + BLK], axis=0)
                for d in range(8):
                    back[d, c * group + g:c * group + g + 1, :] = values[d:d + 1]
        start_eight(back_plan)

        for z in range(zblocks):
            p = z * BLK
            index = irow[:, :, :, p:p + BLK].reshape(ki * cells, BLK)
            got = pick(index, index[:, 0:1] // BLK, coarse_two)
            got = got.reshape(ki, cx, cy, BLK) * ival[:, :, :, p:p + BLK]
            field[2, 1:cx + 1, :, p:p + BLK] = (
                field[1, 1:cx + 1, :, p:p + BLK] + jnp.sum(got, axis=0)
            )
        wait_eight(back_plan)

        fold_rows = lax.broadcasted_iota(jnp.int32, (64, BLK), 0)
        fold_lanes = lax.broadcasted_iota(jnp.int32, (64, BLK), 1)
        fold_index = (fold_lanes % 16) * 8 + fold_rows % 8
        fold_keep = fold_lanes // 16 == fold_rows // 8

        def spread_some(s, carry):
            p = pl.multiple_of(s * BLK, BLK)
            values = jnp.concatenate(
                [returned[d, pl.ds(s, 1), :] for d in range(8)], axis=0
            )
            values = jnp.where(lanes + p < count_ref[...], values, 0.0)
            within = cell[:, pl.ds(p, BLK)] & (BLK - 1)
            upper, lower = within // 16, within % 16
            coarse_part = jnp.concatenate(
                [jnp.where(upper == h, values, 0.0) for h in range(8)], axis=0
            )
            high = coarse_part.astype(jnp.bfloat16)
            low = (coarse_part - high.astype(jnp.float32)).astype(jnp.bfloat16)
            fine_part = jnp.concatenate(
                [jnp.where(lower == l, 1.0, 0.0) for l in range(16)], axis=0
            ).astype(jnp.bfloat16)
            out = lax.dot_general(
                jnp.concatenate([high, low], axis=0), fine_part,
                (((1,), (1,)), ((), ())), preferred_element_type=jnp.float32,
            )
            out = jnp.take_along_axis(
                out[:64] + out[64:], fold_index, axis=1, mode="promise_in_bounds"
            )
            out = jnp.where(fold_keep, out, 0.0).reshape(8, 8, BLK)
            spread[pl.ds(pl.multiple_of(s * 8, 8), 8)] = jnp.sum(out, axis=0)
            return carry

        lax.fori_loop(0, slots, spread_some, 0, unroll=32)
        both = jnp.dot(
            choose[...], split_two(spread[...]), preferred_element_type=jnp.float32
        )
        added = both[:, :BLK] + both[:, BLK:]
        for z in range(zblocks):
            p = z * BLK
            field[2, 1:cx + 1, :, p:p + BLK] = (
                field[2, 1:cx + 1, :, p:p + BLK]
                + added[z * cells:(z + 1) * cells].reshape(cx, cy, BLK)
            )
        for i in range(cx):
            value = field[2, i + 1]
            ysend[2, 0, i:i + 1, :] = value[0:1]
            ysend[2, 1, i:i + 1, :] = value[cy - 1:cy]
        start_halo(2)
        residual_inside(2)
        wait_halo(2)

        for i in range(cx):
            put(3, i, residual_row(2, i))
        start_halo(3)
        smoother_inside(3, 2)
        wait_halo(3)
        for i in range(cx):
            value = smoother_row(3, i)
            put(4, i, value)
            sol_ref[i] = value
        start_halo(4)
        residual_inside(4)
        wait_halo(4)
        for i in range(cx):
            res_ref[i] = residual_row(4, i)

        for t in range(5):
            for s in range(4):
                @pl.when(side_exists[s])
                def _():
                    halo_copy(t, s).wait_send()
        for plan in (slot_plan, back_plan, rim_plan(0), rim_plan(1), rim_plan(2)):
            for d in range(8):
                @pl.when(exists[d])
                def _():
                    eight_copy(*plan, d).wait_send()

    f32, i32, bf16 = jnp.float32, jnp.int32, jnp.bfloat16
    vm = pltpu.VMEM
    dma = pltpu.SemaphoreType.DMA
    scratch = [
        vm((5, cx + 2, cy, nz), f32), vm((5, 2, cx, nz), f32), vm((5, 2, cx, nz), f32),
        vm((cx, cy, nz), f32), vm((cx, cy, nz), f32), vm((6, cx, cy, nz), f32),
        vm((8, cap), i32), vm((kr, crows, BLK), i32), vm((kr, crows, BLK), f32),
        vm((ka, crows, BLK), i32), vm((crows, BLK), f32), vm((ka, crows, BLK), f32),
        vm((crows, BLK), f32), vm((ka, crows, BLK), f32),
        vm((ki, 8, cap), i32), vm((ki, 8, cap), f32),
        vm((ki, cx, cy, nz), i32), vm((ki, cx, cy, nz), f32),
        vm((cx, cy, nz), f32), vm((fine_rows, 2 * BLK), bf16),
        vm((fine_rows, 8 * slots), bf16),
        vm((8, slots, BLK), f32), vm((8, slots, BLK), f32),
        vm((8, slots, BLK), f32), vm((8, slots, BLK), f32),
        vm((3, crows, BLK), f32), vm((3, 8, rim_rows, BLK), f32),
        vm((8 * slots, BLK), f32), vm((cx, cy, nz), f32),
        dma((16,)), dma((5, 4)), dma((5, 4)), dma((8,)), dma((8,)), dma((8,)), dma((8,)),
        dma((3, 8)), dma((3, 8)),
    ]
    whole = pl.BlockSpec(memory_space=pltpu.VMEM)
    in_hbm = pl.BlockSpec(memory_space=pltpu.HBM)
    return pl.pallas_call(
        kernel,
        out_shape=(
            jax.ShapeDtypeStruct((cx, cy, nz), f32),
            jax.ShapeDtypeStruct((cx, cy, nz), f32),
        ),
        in_specs=[in_hbm] * 4 + [whole] + [in_hbm] * 12,
        out_specs=(whole, whole),
        scratch_shapes=scratch,
        compiler_params=pltpu.CompilerParams(
            collective_id=0, has_side_effects=True, vmem_limit_bytes=40 * 1024 * 1024
        ),
        name="vcycle",
    )


def body(
    rhs, diag, smoother_center, smoother_faces, send_count, send_cell, restrict_col,
    restrict_vals, coarse_col, coarse_diag, coarse_vals, csmooth_diag, csmooth_vals,
    remote_row, remote_vals, interp_row, interp_vals,
):
    def rows(array):
        return array.reshape(array.shape[0], -1, BLK)

    cap = send_cell.shape[-1]
    ki = remote_row.shape[0]
    def in_hbm(array):
        return pltpu.with_memory_space_constraint(array, pltpu.HBM)

    operands = (
        rhs, diag, smoother_center, smoother_faces,
        jnp.broadcast_to(send_count.reshape(8, 1), (8, BLK)),
        send_cell.reshape(8, cap), rows(restrict_col), rows(restrict_vals),
        rows(coarse_col), coarse_diag.reshape(-1, BLK), rows(coarse_vals),
        csmooth_diag.reshape(-1, BLK), rows(csmooth_vals),
        remote_row.reshape(ki, 8, cap), remote_vals.reshape(ki, 8, cap),
        interp_row, interp_vals,
    )
    shapes = {
        "rhs": rhs.shape, "send_cell": (8, cap), "restrict_col": operands[6].shape,
        "coarse_col": operands[8].shape, "interp_row": interp_row.shape,
    }
    sizes = (lax.axis_size("gx"), lax.axis_size("gy"))
    operands = [x if n == 4 else in_hbm(x) for n, x in enumerate(operands)]
    return make_kernel(sizes, shapes)(*operands)


def solution(mesh):
    fine = P("gx", "gy", None)
    listed = P(None, "gx", "gy", None)
    placed = (
        fine, fine, fine, listed, fine, P("gx", "gy", None, None), listed, listed,
        listed, fine, listed, fine, listed,
        P(None, "gx", "gy", None, None), P(None, "gx", "gy", None, None),
        listed, listed,
    )
    return jax.shard_map(
        body, mesh=mesh, in_specs=placed, out_specs=(fine, fine), check_vma=False
    )
```

profile of v0, /device:TPU:0, one launch (start us, length us, event | category | flops | bytes accessed | tf_op | source)
XLA Modules:
  0.0 44.0 jit_solution(3721589901839292966)
XLA Ops:
  0.6 0.0 copy-start
  0.6 0.6 %copy-done = s32[1,1,8]{2,1,0:T(1,128)S(1)} copy-done((s32[1,1,8]{2,1,0:T(1,128)S(1)}, s32[1,1,8]{2,1,0:T(1,128)}, u32[]{:S(2)}) %copy-start) | copy-done | bytes 56
  1.3 0.1 broadcast_in_dim.8.count_ref
  1.4 41.3 %vcycle.1 = (f32[8,8,512]{2,1,0:T(8,128)S(1)}, f32[8,8,512]{2,1,0:T(8,128)S(1)}) custom-call(f32[8,8,512]{2,1,0:T(8,128)} %rhs_h.1, f32[8,8,512]{2,1,0:T(8,128)} %diag_h.1, f32[8,8,512]{2,1,0:T(8,128)} %center_h.1, f32[6,8,8,512]{3,2,1,0:T(8,128)} %faces_h.1, s32[8,128]{1,0:T(8,128)S(1)} %broadcast_in_dim.8.count_ref, s32[8,4096]{1,0:T(8,128)} %bitcast.18, ...), custom_call_target="tpu_custom_call" | custom-call | tf_op jit(solution)/shard_map/vcycle/pallas_call | solution.py:518
  42.7 0.7 %copy.21 = f32[8,8,512]{2,1,0:T(8,128)} copy(f32[8,8,512]{2,1,0:T(8,128)S(1)} %get-tuple-element.4) | data formatting | bytes 262144
  43.4 0.7 %copy.22 = f32[8,8,512]{2,1,0:T(8,128)} copy(f32[8,8,512]{2,1,0:T(8,128)S(1)} %get-tuple-element.5) | data formatting | bytes 262144
Async XLA Ops:
  0.6 0.7 %copy-start = (s32[1,1,8]{2,1,0:T(1,128)S(1)}, s32[1,1,8]{2,1,0:T(1,128)}, u32[]{:S(2)}) copy-start(s32[1,1,8]{2,1,0:T(1,128)} %param.21) | copy-start | bytes 100
where the time goes:
time: 44.4 us; the launch traced here: 44 us
  Pallas kernels  41.3 us (93%)
  local copies, waits for them, and re-layouts  2.03 us (5%)
  between operations  0.65 us (1%)
    pallas_call x1, Pallas kernels, body(): return make_kernel(sizes, shapes)(*operands)  41.3 us
    unnamed x4, local copies, waits for them, and re-layouts  1.96 us

commit v1 on v0

--- a/solution.py
+++ b/solution.py
@@ -8,6 +8,7 @@
 BLK = 128
 OFFSETS = ((-1, -1), (-1, 0), (-1, 1), (0, -1), (0, 1), (1, -1), (1, 0), (1, 1))
 SIDES = ((-1, 0), (1, 0), (0, -1), (0, 1))
+CORNERS = (0, 2, 5, 7)
 MESH_ID = pl.DeviceIdType.MESH
 
 
@@ -50,17 +51,25 @@
         rhs_h, diag_h, center_h, faces_h, count_ref, cell_h, rcol_h, rval_h, ccol_h,
         cdiag_h, cval_h, mdiag_h, mval_h, rrow_h, rrval_h, irow_h, ival_h,
         sol_ref, res_ref,
-        field, ysend, yrecv, diag, center, faces, cell, rcol, rval, ccol, cdiag, cval,
+        field, yrecv, diag, center, faces, edges, cell, rcol, rval, ccol, cdiag, cval,
         mdiag, mval, rrow, rrval, irow, ival, resid, fine_two, choose, sent, received,
         back, returned, coarse, rim, spread, partial,
-        in_sem, halo_send, halo_recv, slot_send, slot_recv, back_send, back_recv,
-        rim_send, rim_recv,
+        first_out, first_in, pre_out, pre_in, last_out, last_in, tip_out, tip_in, edges_in,
+        in_sem, first_send, first_recv, pre_send, pre_recv, last_send, last_recv,
+        tip_send, tip_recv, edges_send, edges_recv,
+        slot_send, slot_recv, back_send, back_recv, rim_send, rim_recv,
     ):
         a = lax.axis_index("gx")
         b = lax.axis_index("gy")
 
         loads = [
             (rhs_h, field.at[0, pl.ds(1, cx)]), (center_h, center), (faces_h, faces),
+            (center_h.at[0], edges.at[0, 0]), (center_h.at[cx - 1], edges.at[1, 0]),
+            (center_h.at[:, 0, :], edges.at[2, 0]), (center_h.at[:, cy - 1, :], edges.at[3, 0]),
+            (faces_h.at[:, 0], edges.at[0, pl.ds(1, 6)]),
+            (faces_h.at[:, cx - 1], edges.at[1, pl.ds(1, 6)]),
+            (faces_h.at[:, :, 0, :], edges.at[2, pl.ds(1, 6)]),
+            (faces_h.at[:, :, cy - 1, :], edges.at[3, pl.ds(1, 6)]),
             (diag_h, diag), (cell_h, cell), (rcol_h, rcol), (rval_h, rval),
             (ccol_h, ccol), (mdiag_h, mdiag), (mval_h, mval), (cdiag_h, cdiag),
             (cval_h, cval), (rrow_h, rrow), (rrval_h, rrval), (irow_h, irow),
@@ -105,11 +114,14 @@
         for s in range(4):
             @pl.when(jnp.logical_not(side_exists[s]))
             def _():
-                for t in range(5):
-                    if s < 2:
-                        field[t, 0 if s == 0 else cx + 1] = jnp.zeros((cy, nz), jnp.float32)
-                    else:
-                        yrecv[t, s - 2] = jnp.zeros((cx, nz), jnp.float32)
+                first_in[s] = jnp.zeros(first_in.shape[1:], jnp.float32)
+                last_in[s] = jnp.zeros(last_in.shape[1:], jnp.float32)
+                edges_in[s] = jnp.zeros(edges_in.shape[1:], jnp.float32)
+        for c in range(4):
+            @pl.when(jnp.logical_not(exists[CORNERS[c]]))
+            def _():
+                pre_in[c] = jnp.zeros(pre_in.shape[1:], jnp.float32)
+                tip_in[c] = jnp.zeros(tip_in.shape[1:], jnp.float32)
         for d in range(8):
             @pl.when(jnp.logical_not(exists[d]))
             def _():
@@ -118,40 +130,75 @@
                 for t in range(3):
                     rim[t, d] = jnp.zeros((rim_rows, BLK), jnp.float32)
 
-        def halo_copy(t, s):
-            dx, dy = SIDES[s]
-            if s == 0:
-                src, dst = field.at[t, 1], field.at[t, cx + 1]
-            elif s == 1:
-                src, dst = field.at[t, cx], field.at[t, 0]
-            else:
-                src, dst = ysend.at[t, s - 2], yrecv.at[t, 3 - s]
-            return pltpu.make_async_remote_copy(
-                src_ref=src, dst_ref=dst, send_sem=halo_send.at[t, s],
-                recv_sem=halo_recv.at[t, s ^ 1],
-                device_id=(a + dx, b + dy), device_id_type=MESH_ID,
-            )
-
-        def halo_arrival(t, s):
-            dx, dy = SIDES[s]
-            dst = field.at[t, 0 if s == 0 else cx + 1] if s < 2 else yrecv.at[t, s - 2]
-            return pltpu.make_async_remote_copy(
-                src_ref=dst, dst_ref=dst, send_sem=halo_send.at[t, s],
-                recv_sem=halo_recv.at[t, s],
-                device_id=(a + dx, b + dy), device_id_type=MESH_ID,
-            )
-
-        def start_halo(t):
-            for s in (2, 3, 0, 1):
-                @pl.when(side_exists[s])
+        def item(cond, step, src, there_ref, here_ref, send, there_sem, here_sem):
+            target = (a + step[0], b + step[1])
+
+            def copy():
+                return pltpu.make_async_remote_copy(
+                    src_ref=src, dst_ref=there_ref, send_sem=send, recv_sem=there_sem,
+                    device_id=target, device_id_type=MESH_ID,
+                )
+
+            def arrival():
+                return pltpu.make_async_remote_copy(
+                    src_ref=here_ref, dst_ref=here_ref, send_sem=send, recv_sem=here_sem,
+                    device_id=target, device_id_type=MESH_ID,
+                )
+
+            return cond, copy, arrival
+
+        def side_items(out, into, send, recv):
+            return [
+                item(
+                    side_exists[s], SIDES[s], out(s), into(s ^ 1), into(s),
+                    send(s), recv(s ^ 1), recv(s),
+                )
+                for s in (2, 3, 0, 1)
+            ]
+
+        def corner_items(out, into, send, recv):
+            return [
+                item(
+                    exists[CORNERS[c]], OFFSETS[CORNERS[c]], out.at[c], into.at[3 - c],
+                    into.at[c], send.at[c], recv.at[3 - c], recv.at[c],
+                )
+                for c in range(4)
+            ]
+
+        first_items = corner_items(pre_out, pre_in, pre_send, pre_recv) + side_items(
+            lambda s: first_out.at[s], lambda s: first_in.at[s],
+            lambda s: first_send.at[s], lambda s: first_recv.at[s],
+        )
+        last_items = corner_items(tip_out, tip_in, tip_send, tip_recv) + side_items(
+            lambda s: last_out.at[s], lambda s: last_in.at[s],
+            lambda s: last_send.at[s], lambda s: last_recv.at[s],
+        )
+
+        def edge_items(t):
+            low, size = ((0, 3), (3, 2), (5, 2))[t]
+            return side_items(
+                lambda s: edges.at[s, pl.ds(low, size)],
+                lambda s: edges_in.at[s, pl.ds(low, size)],
+                lambda s: edges_send.at[t, s], lambda s: edges_recv.at[t, s],
+            )
+
+        def start_items(items):
+            for cond, copy, _ in items:
+                @pl.when(cond)
                 def _():
-                    halo_copy(t, s).start()
-
-        def wait_halo(t):
-            for s in range(4):
-                @pl.when(side_exists[s])
+                    copy().start()
+
+        def wait_items(items):
+            for cond, _, arrival in items:
+                @pl.when(cond)
                 def _():
-                    halo_arrival(t, s).wait_recv()
+                    arrival().wait_recv()
+
+        def finish_items(items):
+            for cond, copy, _ in items:
+                @pl.when(cond)
+                def _():
+                    copy().wait_send()
 
         def eight_copy(src, dst, send_sem, recv_sem, d):
             dx, dy = OFFSETS[d]
@@ -251,19 +298,76 @@
                     out = out + faces[q, i] * one
             return out
 
-        def put(t, i, value):
-            field[t, i + 1] = value
-            ysend[t, 0, i:i + 1, :] = value[0:1]
-            ysend[t, 1, i:i + 1, :] = value[cy - 1:cy]
-
-        loads[0].wait()
-        for i in range(cx):
-            value = field[0, i + 1]
-            ysend[0, 0, i:i + 1, :] = value[0:1]
-            ysend[0, 1, i:i + 1, :] = value[cy - 1:cy]
+        def put_edges(out, n, i, value):
+            base = n * zblocks * 8
+            for z in range(zblocks):
+                part = value[:, z * BLK:(z + 1) * BLK]
+                row = base + z * 8
+                if i == 0:
+                    out[0, row:row + 8, :] = part
+                if i == cx - 1:
+                    out[1, row:row + 8, :] = part
+                out[2, row + i:row + i + 1, :] = part[0:1]
+                out[3, row + i:row + i + 1, :] = part[cy - 1:cy]
+
+        def layer(ref, s, n):
+            base = n * zblocks * 8
+            return jnp.concatenate(
+                [ref[s, base + 8 * z:base + 8 * z + 8, :] for z in range(zblocks)], axis=1
+            )
+
+        def column(ref, c, low, step=1):
+            return jnp.concatenate(
+                [ref[c, low + z * step:low + z * step + 1, :] for z in range(zblocks)], axis=1
+            )
+
+        def put_column(ref, c, low, value):
+            for z in range(zblocks):
+                ref[c, low + z:low + z + 1, :] = value[:, z * BLK:(z + 1) * BLK]
+
+        def corner_cell(c):
+            dx, dy = OFFSETS[CORNERS[c]]
+            return (0 if dx < 0 else cx - 1), (0 if dy < 0 else cy - 1), -dx, -dy
+
+        away = [1 + s for s in range(4)]
+        facing = [1 + (s ^ 1) for s in range(4)]
+        along = [(3, 4), (3, 4), (1, 2), (1, 2)]
+        ends = [(0, 1), (2, 3), (0, 2), (1, 3)]
+        first_row, last_row = row_ids == 0, row_ids == cy - 1
+
+        def at_ends(low, high):
+            wide = (cy, nz)
+            return jnp.where(
+                first_row, jnp.broadcast_to(low, wide),
+                jnp.where(last_row, jnp.broadcast_to(high, wide), 0.0),
+            )
+
+        for load in loads[0:3]:
+            load.wait()
+        smoother_inside(0, None)
+        for i in range(cx):
+            put_edges(first_out, 0, i, field[0, i + 1])
+            put_edges(first_out, 1, i, partial[i])
+        for c in range(4):
+            i, j, _, _ = corner_cell(c)
+            put_column(pre_out, c, 0, field[0, i + 1][j:j + 1])
+        for load in loads[3:11]:
+            load.wait()
+        end_row = 3 * zblocks * 8
+        for s in range(4):
+            face = edges[s, 1 + s]
+            low, high = along[s]
+            at_low, at_high = edges[s, low][0:1], edges[s, high][cy - 1:cy]
+            for z in range(zblocks):
+                row = 2 * zblocks * 8 + z * 8
+                first_out[s, row:row + 8, :] = face[:, z * BLK:(z + 1) * BLK]
+                first_out[s, end_row + z:end_row + z + 1, :] = at_low[:, z * BLK:(z + 1) * BLK]
+                row = end_row + zblocks + z
+                first_out[s, row:row + 1, :] = at_high[:, z * BLK:(z + 1) * BLK]
         pl.semaphore_wait(barrier, total)
-        start_halo(0)
-        for load in loads[1:5]:
+        start_items(first_items)
+        loads = loads[10:]
+        for load in loads[1:3]:
             load.wait()
 
         cell_index = jnp.concatenate(
@@ -276,16 +380,29 @@
         fine_ids = lax.broadcasted_iota(jnp.int32, (fine_rows, 8 * slots), 0)
         choose[...] = jnp.where(fine_ids == across, 1.0, 0.0).astype(jnp.bfloat16)
 
-        smoother_inside(0, None)
-        wait_halo(0)
-        for i in range(cx):
-            put(1, i, smoother_row(0, i))
-        start_halo(1)
+        for load in loads[3:]:
+            load.wait()
+        wait_items(first_items)
+
+        def set_ghost(t, s, value):
+            if s < 2:
+                field[t, 0 if s == 0 else cx + 1] = value
+            else:
+                yrecv[t, s - 2] = value
+
+        for s in range(4):
+            set_ghost(0, s, layer(first_in, s, 0))
+            low, high = ends[s]
+            set_ghost(1, s, (
+                layer(first_in, s, 1) + layer(first_in, s, 2) * layer(first_out, s, 0)
+                + at_ends(
+                    column(first_in, s, end_row) * column(pre_in, low, 0),
+                    column(first_in, s, end_row + zblocks) * column(pre_in, high, 0),
+                )
+            ))
+        for i in range(cx):
+            field[1, i + 1] = smoother_row(0, i)
         residual_inside(1)
-        for load in loads[5:]:
-            load.wait()
-
-        wait_halo(1)
         for i in range(cx):
             resid[i] = residual_row(1, i)
         table = jnp.concatenate(
@@ -327,6 +444,7 @@
         def coarse_apply(t, vector, diagonal, values):
             coarse[t] = vector
             start_eight(rim_plan(t))
+            start_items(edge_items(t))
             index = ccol[...].reshape(ka * crows, BLK)
             got = pick(index, index[:, 0:1] // BLK, split_two(vector))
             own = diagonal[...] * vector + jnp.sum(
@@ -415,34 +533,91 @@
                 field[2, 1:cx + 1, :, p:p + BLK]
                 + added[z * cells:(z + 1) * cells].reshape(cx, cy, BLK)
             )
-        for i in range(cx):
-            value = field[2, i + 1]
-            ysend[2, 0, i:i + 1, :] = value[0:1]
-            ysend[2, 1, i:i + 1, :] = value[cy - 1:cy]
-        start_halo(2)
         residual_inside(2)
-        wait_halo(2)
-
-        for i in range(cx):
-            put(3, i, residual_row(2, i))
-        start_halo(3)
+        for i in range(cx):
+            field[3, i + 1] = partial[i]
         smoother_inside(3, 2)
-        wait_halo(3)
+        for i in range(cx):
+            put_edges(last_out, 0, i, field[2, i + 1])
+            put_edges(last_out, 1, i, field[3, i + 1])
+            put_edges(last_out, 2, i, partial[i])
+        for c in range(4):
+            i, j, di, dj = corner_cell(c)
+            put_column(tip_out, c, 0, field[2, i + 1][j:j + 1])
+            put_column(tip_out, c, zblocks, field[2, i + 1][j + dj:j + dj + 1])
+            put_column(tip_out, c, 2 * zblocks, field[2, i + 1 + di][j:j + 1])
+            put_column(tip_out, c, 3 * zblocks, field[3, i + 1][j:j + 1])
+        start_items(last_items)
+        for t in range(3):
+            wait_items(edge_items(t))
+        wait_items(last_items)
+
+        beyond = [layer(last_in, s, 0) for s in range(4)]
+        for s in range(4):
+            set_ghost(2, s, beyond[s])
+        corner_resid = []
+        for c in range(4):
+            i, j, _, _ = corner_cell(c)
+            sx, sy = (0 if i == 0 else 1), (2 if j == 0 else 3)
+            value = (
+                column(tip_in, c, 3 * zblocks) + beyond[sx][j:j + 1] + beyond[sy][i:i + 1]
+            )
+            corner_resid.append(jnp.where(exists[CORNERS[c]], value, 0.0))
+
+        for s in range(4):
+            low, high = ends[s]
+            low_face, high_face = along[s]
+            place = 0 if s % 2 == 0 else cy - 1
+            low_side, high_side = (2, 3) if s < 2 else (0, 1)
+            change = layer(last_out, s, 0) + at_ends(
+                column(tip_in, low, 0), column(tip_in, high, 0)
+            )
+            beyond_resid = jnp.where(
+                side_exists[s], layer(last_in, s, 1) + change, 0.0
+            )
+            set_ghost(3, s, beyond_resid)
+            own_resid = layer(last_out, s, 1) + beyond[s] + at_ends(
+                beyond[low_side][place:place + 1], beyond[high_side][place:place + 1]
+            )
+            wide = (cy, nz)
+            before = jnp.where(
+                first_row, jnp.broadcast_to(corner_resid[low], wide), pltpu.roll(change, 1, 0)
+            )
+            after = jnp.where(
+                last_row, jnp.broadcast_to(corner_resid[high], wide),
+                pltpu.roll(change, cy - 1, 0),
+            )
+            column_low = zblocks if s >= 2 else 2 * zblocks
+            second = at_ends(
+                column(tip_in, low, column_low), column(tip_in, high, column_low)
+            )
+            set_ghost(4, s, (
+                layer(last_in, s, 2)
+                + edges_in[s, 0] * change
+                + edges_in[s, low_face] * before
+                + edges_in[s, high_face] * after
+                + edges_in[s, facing[s]] * own_resid
+                + edges_in[s, away[s]] * second
+                + edges_in[s, 5] * jnp.where(lane_ids == 0, 0.0, pltpu.roll(change, 1, 1))
+                + edges_in[s, 6] * jnp.where(lane_ids == nz - 1, 0.0, pltpu.roll(change, nz - 1, 1))
+            ))
+        for i in range(cx):
+            partial[i] = field[3, i + 1]
+        for i in range(cx):
+            field[3, i + 1] = residual_row(2, i)
+        smoother_inside(3, 2)
         for i in range(cx):
             value = smoother_row(3, i)
-            put(4, i, value)
+            field[4, i + 1] = value
             sol_ref[i] = value
-        start_halo(4)
         residual_inside(4)
-        wait_halo(4)
         for i in range(cx):
             res_ref[i] = residual_row(4, i)
 
-        for t in range(5):
-            for s in range(4):
-                @pl.when(side_exists[s])
-                def _():
-                    halo_copy(t, s).wait_send()
+        finish_items(first_items)
+        finish_items(last_items)
+        for t in range(3):
+            finish_items(edge_items(t))
         for plan in (slot_plan, back_plan, rim_plan(0), rim_plan(1), rim_plan(2)):
             for d in range(8):
                 @pl.when(exists[d])
@@ -453,8 +628,9 @@
     vm = pltpu.VMEM
     dma = pltpu.SemaphoreType.DMA
     scratch = [
-        vm((5, cx + 2, cy, nz), f32), vm((5, 2, cx, nz), f32), vm((5, 2, cx, nz), f32),
+        vm((5, cx + 2, cy, nz), f32), vm((5, 2, cx, nz), f32),
         vm((cx, cy, nz), f32), vm((cx, cy, nz), f32), vm((6, cx, cy, nz), f32),
+        vm((4, 7, 8, nz), f32),
         vm((8, cap), i32), vm((kr, crows, BLK), i32), vm((kr, crows, BLK), f32),
         vm((ka, crows, BLK), i32), vm((crows, BLK), f32), vm((ka, crows, BLK), f32),
         vm((crows, BLK), f32), vm((ka, crows, BLK), f32),
@@ -466,7 +642,14 @@
         vm((8, slots, BLK), f32), vm((8, slots, BLK), f32),
         vm((3, crows, BLK), f32), vm((3, 8, rim_rows, BLK), f32),
         vm((8 * slots, BLK), f32), vm((cx, cy, nz), f32),
-        dma((16,)), dma((5, 4)), dma((5, 4)), dma((8,)), dma((8,)), dma((8,)), dma((8,)),
+        vm((4, (3 * 8 + 2) * zblocks, BLK), f32), vm((4, (3 * 8 + 2) * zblocks, BLK), f32),
+        vm((4, zblocks, BLK), f32), vm((4, zblocks, BLK), f32),
+        vm((4, 3 * 8 * zblocks, BLK), f32), vm((4, 3 * 8 * zblocks, BLK), f32),
+        vm((4, 4 * zblocks, BLK), f32), vm((4, 4 * zblocks, BLK), f32),
+        vm((4, 7, 8, nz), f32),
+        dma((24,)), dma((4,)), dma((4,)), dma((4,)), dma((4,)), dma((4,)), dma((4,)),
+        dma((4,)), dma((4,)), dma((3, 4)), dma((3, 4)),
+        dma((8,)), dma((8,)), dma((8,)), dma((8,)),
         dma((3, 8)), dma((3, 8)),
     ]
     whole = pl.BlockSpec(memory_space=pltpu.VMEM)

time: 44.4 us -> 38.5 us (0.87)
  Pallas kernels: 41.3 us -> 35.7 us
    pallas_call x1, Pallas kernels: 41.3 us -> 35.7 us  [body(): return make_kernel(sizes, shapes)(*operands)]
where the time goes in v1:
time: 38.5 us; the launch traced here: 38.3 us
  Pallas kernels  35.7 us (93%)
  local copies, waits for them, and re-layouts  2.03 us (5%)
  between operations  0.65 us (2%)
    pallas_call x1, Pallas kernels, body(): return make_kernel(sizes, shapes)(*operands)  35.7 us
    unnamed x4, local copies, waits for them, and re-layouts  1.96 us

profile of v1, /device:TPU:0, one launch (start us, length us, event | category | flops | bytes accessed | tf_op | source)
XLA Modules:
  0.0 38.3 jit_solution(17161557414093162495)
XLA Ops:
  0.6 0.0 copy-start
  0.6 0.6 %copy-done = s32[1,1,8]{2,1,0:T(1,128)S(1)} copy-done((s32[1,1,8]{2,1,0:T(1,128)S(1)}, s32[1,1,8]{2,1,0:T(1,128)}, u32[]{:S(2)}) %copy-start) | copy-done | bytes 56
  1.3 0.1 broadcast_in_dim.8.count_ref
  1.4 35.7 %vcycle.1 = (f32[8,8,512]{2,1,0:T(8,128)S(1)}, f32[8,8,512]{2,1,0:T(8,128)S(1)}) custom-call(f32[8,8,512]{2,1,0:T(8,128)} %rhs_h.1, f32[8,8,512]{2,1,0:T(8,128)} %diag_h.1, f32[8,8,512]{2,1,0:T(8,128)} %center_h.1, f32[6,8,8,512]{3,2,1,0:T(8,128)} %faces_h.1, s32[8,128]{1,0:T(8,128)S(1)} %broadcast_in_dim.8.count_ref, s32[8,4096]{1,0:T(8,128)} %bitcast.18, ...), custom_call_target="tpu_custom_call" | custom-call | tf_op jit(solution)/shard_map/vcycle/pallas_call | solution.py:701
  37.0 0.7 %copy.21 = f32[8,8,512]{2,1,0:T(8,128)} copy(f32[8,8,512]{2,1,0:T(8,128)S(1)} %get-tuple-element.4) | data formatting | bytes 262144
  37.7 0.7 %copy.22 = f32[8,8,512]{2,1,0:T(8,128)} copy(f32[8,8,512]{2,1,0:T(8,128)S(1)} %get-tuple-element.5) | data formatting | bytes 262144
Async XLA Ops:
  0.6 0.7 %copy-start = (s32[1,1,8]{2,1,0:T(1,128)S(1)}, s32[1,1,8]{2,1,0:T(1,128)}, u32[]{:S(2)}) copy-start(s32[1,1,8]{2,1,0:T(1,128)} %param.21) | copy-start | bytes 100

commit v2 on v1

v2 whole, which is shorter than its diff:
```python
import jax
import jax.numpy as jnp
from jax import lax
from jax.experimental import pallas as pl
from jax.experimental.pallas import tpu as pltpu
from jax.sharding import PartitionSpec as P

BLK = 128
OFFSETS = ((-1, -1), (-1, 0), (-1, 1), (0, -1), (0, 1), (1, -1), (1, 0), (1, 1))
SIDES = ((-1, 0), (1, 0), (0, -1), (0, 1))
CORNERS = (0, 2, 5, 7)
MESH_ID = pl.DeviceIdType.MESH


def split_two(table):
    high = table.astype(jnp.bfloat16)
    low = (table - high.astype(jnp.float32)).astype(jnp.bfloat16)
    return jnp.concatenate([high, low], axis=1)


def one_hot(base, width):
    ids = lax.broadcasted_iota(jnp.int32, (base.shape[0], width), 1)
    return jnp.where(ids == base, 1.0, 0.0).astype(jnp.bfloat16)


def pick(index, base, table_two):
    return pick_hot(index, one_hot(base, table_two.shape[0]), table_two)


def pick_hot(index, hot, table_two):
    both = jnp.dot(hot, table_two, preferred_element_type=jnp.float32)
    rows = both[:, :BLK] + both[:, BLK:]
    return jnp.take_along_axis(rows, index & (BLK - 1), axis=1, mode="promise_in_bounds")


def make_kernel(sizes, shapes):
    na, nb = sizes
    cx, cy, nz = shapes["rhs"]
    zblocks = nz // BLK
    cells = cx * cy
    fine_rows = cells * zblocks
    cap = shapes["send_cell"][1]
    slots = cap // BLK
    kr, crows, _ = shapes["restrict_col"]
    ka = shapes["coarse_col"][0]
    ki = shapes["interp_row"][0]
    rim_rows = 8

    def fine_place(block):
        return (block % zblocks) * cells + block // zblocks

    def kernel(
        rhs_h, diag_h, center_h, faces_h, count_h, cell_h, rcol_h, rval_h, ccol_h,
        cdiag_h, cval_h, mdiag_h, mval_h, rrow_h, rrval_h, irow_h, ival_h,
        sol_ref, res_ref,
        hot_back, hot_spread, count, counts, field, yrecv, diag, center, faces, edges, cell, rcol, rval, ccol, cdiag, cval,
        mdiag, mval, rrow, rrval, irow, ival, resid, fine_two, choose, sent, received,
        back, returned, coarse, rim, spread, partial,
        first_out, first_in, pre_out, pre_in, last_out, last_in, tip_out, tip_in, edges_in,
        in_sem, first_send, first_recv, pre_send, pre_recv, last_send, last_recv,
        tip_send, tip_recv, edges_send, edges_recv,
        slot_send, slot_recv, back_send, back_recv, rim_send, rim_recv,
    ):
        a = lax.axis_index("gx")
        b = lax.axis_index("gy")

        loads = [
            (rhs_h, field.at[0, pl.ds(1, cx)]), (center_h, center), (faces_h, faces),
            (center_h.at[0], edges.at[0, 0]), (center_h.at[cx - 1], edges.at[1, 0]),
            (center_h.at[:, 0, :], edges.at[2, 0]), (center_h.at[:, cy - 1, :], edges.at[3, 0]),
            (faces_h.at[:, 0], edges.at[0, pl.ds(1, 6)]),
            (faces_h.at[:, cx - 1], edges.at[1, pl.ds(1, 6)]),
            (faces_h.at[:, :, 0, :], edges.at[2, pl.ds(1, 6)]),
            (faces_h.at[:, :, cy - 1, :], edges.at[3, pl.ds(1, 6)]),
            (diag_h, diag), (cell_h, cell), (count_h, count), (rcol_h, rcol), (rval_h, rval),
            (ccol_h, ccol), (mdiag_h, mdiag), (mval_h, mval), (cdiag_h, cdiag),
            (cval_h, cval), (rrow_h, rrow), (rrval_h, rrval), (irow_h, irow),
            (ival_h, ival),
        ]
        loads = [
            pltpu.make_async_copy(source, target, in_sem.at[n])
            for n, (source, target) in enumerate(loads)
        ]

        def there(step):
            dx, dy = step
            checks = []
            if dx < 0:
                checks.append(a > 0)
            if dx > 0:
                checks.append(a < na - 1)
            if dy < 0:
                checks.append(b > 0)
            if dy > 0:
                checks.append(b < nb - 1)
            out = checks[0]
            for check in checks[1:]:
                out = jnp.logical_and(out, check)
            return out

        exists = [there(step) for step in OFFSETS]
        side_exists = [there(step) for step in SIDES]

        barrier = pltpu.get_barrier_semaphore()
        total = jnp.int32(0)
        for d, (dx, dy) in enumerate(OFFSETS):
            @pl.when(exists[d])
            def _():
                pl.semaphore_signal(
                    barrier, inc=1, device_id=(a + dx, b + dy), device_id_type=MESH_ID
                )
            total = total + exists[d].astype(jnp.int32)

        for load in loads[:3]:
            load.start()

        def item(cond, step, src, there_ref, here_ref, send, there_sem, here_sem):
            target = (a + step[0], b + step[1])

            def copy():
                return pltpu.make_async_remote_copy(
                    src_ref=src, dst_ref=there_ref, send_sem=send, recv_sem=there_sem,
                    device_id=target, device_id_type=MESH_ID,
                )

            def arrival():
                return pltpu.make_async_remote_copy(
                    src_ref=here_ref, dst_ref=here_ref, send_sem=send, recv_sem=here_sem,
                    device_id=target, device_id_type=MESH_ID,
                )

            return cond, copy, arrival

        def side_items(out, into, send, recv):
            return [
                item(
                    side_exists[s], SIDES[s], out(s), into(s ^ 1), into(s),
                    send(s), recv(s ^ 1), recv(s),
                )
                for s in (2, 3, 0, 1)
            ]

        def corner_items(out, into, send, recv):
            return [
                item(
                    exists[CORNERS[c]], OFFSETS[CORNERS[c]], out.at[c], into.at[3 - c],
                    into.at[c], send.at[c], recv.at[3 - c], recv.at[c],
                )
                for c in range(4)
            ]

        first_items = corner_items(pre_out, pre_in, pre_send, pre_recv) + side_items(
            lambda s: first_out.at[s], lambda s: first_in.at[s],
            lambda s: first_send.at[s], lambda s: first_recv.at[s],
        )
        part = 8 * zblocks
        early_items = side_items(
            lambda s: last_out.at[s, pl.ds(0, part)], lambda s: last_in.at[s, pl.ds(0, part)],
            lambda s: last_send.at[0, s], lambda s: last_recv.at[0, s],
        )
        last_items = corner_items(tip_out, tip_in, tip_send, tip_recv) + side_items(
            lambda s: last_out.at[s, pl.ds(part, 2 * part)],
            lambda s: last_in.at[s, pl.ds(part, 2 * part)],
            lambda s: last_send.at[1, s], lambda s: last_recv.at[1, s],
        )

        def edge_items(t):
            low, size = ((0, 3), (3, 2), (5, 2))[t]
            return side_items(
                lambda s: edges.at[s, pl.ds(low, size)],
                lambda s: edges_in.at[s, pl.ds(low, size)],
                lambda s: edges_send.at[t, s], lambda s: edges_recv.at[t, s],
            )

        def start_items(items):
            for cond, copy, _ in items:
                @pl.when(cond)
                def _():
                    copy().start()

        def wait_items(items):
            for cond, _, arrival in items:
                @pl.when(cond)
                def _():
                    arrival().wait_recv()

        def finish_items(items):
            for cond, copy, _ in items:
                @pl.when(cond)
                def _():
                    copy().wait_send()

        def eight_copy(src, dst, send_sem, recv_sem, d):
            dx, dy = OFFSETS[d]
            return pltpu.make_async_remote_copy(
                src_ref=src(d), dst_ref=dst(7 - d), send_sem=send_sem(d),
                recv_sem=recv_sem(7 - d),
                device_id=(a + dx, b + dy), device_id_type=MESH_ID,
            )

        def eight_arrival(dst, send_sem, recv_sem, d):
            dx, dy = OFFSETS[d]
            return pltpu.make_async_remote_copy(
                src_ref=dst(d), dst_ref=dst(d), send_sem=send_sem(d), recv_sem=recv_sem(d),
                device_id=(a + dx, b + dy), device_id_type=MESH_ID,
            )

        slot_plan = (
            lambda d: sent.at[d], lambda d: received.at[d],
            lambda d: slot_send.at[d], lambda d: slot_recv.at[d],
        )
        back_plan = (
            lambda d: back.at[d], lambda d: returned.at[d],
            lambda d: back_send.at[d], lambda d: back_recv.at[d],
        )

        def rim_plan(t):
            return (
                lambda d: coarse.at[t, pl.ds(0, rim_rows)], lambda d: rim.at[t, d],
                lambda d: rim_send.at[t, d], lambda d: rim_recv.at[t, d],
            )

        def start_eight(plan):
            for d in (0, 2, 5, 7, 3, 4, 1, 6):
                @pl.when(exists[d])
                def _():
                    eight_copy(*plan, d).start()

        def wait_eight(plan):
            for d in range(8):
                @pl.when(exists[d])
                def _():
                    eight_arrival(*plan[1:], d).wait_recv()

        row_ids = lax.broadcasted_iota(jnp.int32, (cy, nz), 0)
        lane_ids = lax.broadcasted_iota(jnp.int32, (cy, nz), 1)

        zeros = jnp.zeros((cy, nz), jnp.float32)

        def beside(t, i):
            centre = field[t, i + 1]
            return centre, [
                field[t, i] if i > 0 else zeros,
                field[t, i + 2] if i < cx - 1 else zeros,
                jnp.where(row_ids == 0, 0.0, pltpu.roll(centre, 1, 0)),
                jnp.where(row_ids == cy - 1, 0.0, pltpu.roll(centre, cy - 1, 0)),
                jnp.where(lane_ids == 0, 0.0, pltpu.roll(centre, 1, 1)),
                jnp.where(lane_ids == nz - 1, 0.0, pltpu.roll(centre, nz - 1, 1)),
            ]

        def sides(t, i):
            out = [
                jnp.where(row_ids == 0, jnp.broadcast_to(yrecv[t, 0, i:i + 1, :], (cy, nz)), 0.0),
                jnp.where(row_ids == cy - 1, jnp.broadcast_to(yrecv[t, 1, i:i + 1, :], (cy, nz)), 0.0),
            ]
            return [
                field[t, 0] if i == 0 else None,
                field[t, cx + 1] if i == cx - 1 else None,
            ] + out

        def residual_inside(t):
            for i in range(cx):
                centre, near = beside(t, i)
                sums = near[0]
                for one in near[1:]:
                    sums = sums + one
                partial[i] = field[0, i + 1] - ((6.0 + diag[i]) * centre - sums)

        def residual_row(t, i):
            out = partial[i]
            for one in sides(t, i):
                if one is not None:
                    out = out + one
            return out

        def smoother_inside(t, base):
            for i in range(cx):
                centre, near = beside(t, i)
                out = center[i] * centre
                for q in range(6):
                    out = out + faces[q, i] * near[q]
                partial[i] = out if base is None else field[base, i + 1] + out

        def smoother_row(t, i):
            out = partial[i]
            for q, one in enumerate(sides(t, i)):
                if one is not None:
                    out = out + faces[q, i] * one
            return out

        def put_edges(out, n, i, value):
            base = n * zblocks * 8
            for z in range(zblocks):
                part = value[:, z * BLK:(z + 1) * BLK]
                row = base + z * 8
                if i == 0:
                    out[0, row:row + 8, :] = part
                if i == cx - 1:
                    out[1, row:row + 8, :] = part
                out[2, row + i:row + i + 1, :] = part[0:1]
                out[3, row + i:row + i + 1, :] = part[cy - 1:cy]

        def layer(ref, s, n):
            base = n * zblocks * 8
            return jnp.concatenate(
                [ref[s, base + 8 * z:base + 8 * z + 8, :] for z in range(zblocks)], axis=1
            )

        def column(ref, c, low, step=1):
            return jnp.concatenate(
                [ref[c, low + z * step:low + z * step + 1, :] for z in range(zblocks)], axis=1
            )

        def put_column(ref, c, low, value):
            for z in range(zblocks):
                ref[c, low + z:low + z + 1, :] = value[:, z * BLK:(z + 1) * BLK]

        def corner_cell(c):
            dx, dy = OFFSETS[CORNERS[c]]
            return (0 if dx < 0 else cx - 1), (0 if dy < 0 else cy - 1), -dx, -dy

        away = [1 + s for s in range(4)]
        facing = [1 + (s ^ 1) for s in range(4)]
        along = [(3, 4), (3, 4), (1, 2), (1, 2)]
        ends = [(0, 1), (2, 3), (0, 2), (1, 3)]
        first_row, last_row = row_ids == 0, row_ids == cy - 1

        def at_ends(low, high):
            wide = (cy, nz)
            return jnp.where(
                first_row, jnp.broadcast_to(low, wide),
                jnp.where(last_row, jnp.broadcast_to(high, wide), 0.0),
            )

        for load in loads[0:3]:
            load.wait()
        smoother_inside(0, None)
        for i in range(cx):
            put_edges(first_out, 0, i, field[0, i + 1])
            put_edges(first_out, 1, i, partial[i])
        for c in range(4):
            i, j, _, _ = corner_cell(c)
            put_column(pre_out, c, 0, field[0, i + 1][j:j + 1])
        end_row = 3 * zblocks * 8
        face_rows = 2 * zblocks * 8
        for z in range(zblocks):
            p = z * BLK
            row = face_rows + z * 8
            first_out[0, row:row + 8, :] = faces[0, 0, :, p:p + BLK]
            first_out[1, row:row + 8, :] = faces[1, cx - 1, :, p:p + BLK]
            for i in range(cx):
                first_out[2, row + i:row + i + 1, :] = faces[2, i, 0:1, p:p + BLK]
                first_out[3, row + i:row + i + 1, :] = faces[3, i, cy - 1:cy, p:p + BLK]
            for s in range(4):
                place = (0 if s % 2 == 0 else (cx if s < 2 else cy) - 1)
                if s < 2:
                    at_low = faces[2, place, 0:1, p:p + BLK]
                    at_high = faces[3, place, cy - 1:cy, p:p + BLK]
                else:
                    at_low = faces[0, 0, place:place + 1, p:p + BLK]
                    at_high = faces[1, cx - 1, place:place + 1, p:p + BLK]
                first_out[s, end_row + z:end_row + z + 1, :] = at_low
                row_high = end_row + zblocks + z
                first_out[s, row_high:row_high + 1, :] = at_high
        pl.semaphore_wait(barrier, total)
        start_items(first_items)
        for load in loads[3:]:
            load.start()
        for s in range(4):
            @pl.when(jnp.logical_not(side_exists[s]))
            def _():
                first_in[s] = jnp.zeros(first_in.shape[1:], jnp.float32)
                last_in[s] = jnp.zeros(last_in.shape[1:], jnp.float32)
                edges_in[s] = jnp.zeros(edges_in.shape[1:], jnp.float32)
        for c in range(4):
            @pl.when(jnp.logical_not(exists[CORNERS[c]]))
            def _():
                pre_in[c] = jnp.zeros(pre_in.shape[1:], jnp.float32)
                tip_in[c] = jnp.zeros(tip_in.shape[1:], jnp.float32)
        for d in range(8):
            @pl.when(jnp.logical_not(exists[d]))
            def _():
                received[d] = jnp.zeros((slots, BLK), jnp.float32)
                returned[d] = jnp.zeros((slots, BLK), jnp.float32)
                for t in range(3):
                    rim[t, d] = jnp.zeros((rim_rows, BLK), jnp.float32)

        edge_loads, loads = loads[3:11], loads[10:]
        for load in loads[1:4]:
            load.wait()
        slot_rows = lax.broadcasted_iota(jnp.int32, (8, BLK), 0)
        value = jnp.zeros((8, BLK), jnp.int32)
        for d in range(8):
            value = jnp.where(slot_rows == d, count[0, 0, d], value)
        counts[...] = value

        cell_index = jnp.concatenate(
            [cell[:, s * BLK:(s + 1) * BLK] for s in range(slots)], axis=0
        )
        cell_base = fine_place(cell_index[:, 0:1] // BLK)
        across = jnp.transpose(
            jnp.broadcast_to(cell_base, (8 * slots, BLK)).astype(jnp.float32)
        )[0:1].astype(jnp.int32)
        fine_ids = lax.broadcasted_iota(jnp.int32, (fine_rows, 8 * slots), 0)
        choose[...] = jnp.where(fine_ids == across, 1.0, 0.0).astype(jnp.bfloat16)
        hot_slot = one_hot(cell_base, fine_rows)

        for load in loads[4:] + edge_loads:
            load.wait()
        group = 8 if slots % 8 == 0 else 1
        batch = group * ki * 8

        def back_index(c):
            parts = [(c * group + g) * BLK for g in range(group)]
            return jnp.concatenate(
                [rrow[:, :, p:p + BLK].reshape(ki * 8, BLK) for p in parts], axis=0
            )

        for c in range(slots // group):
            hot_back[c * batch:(c + 1) * batch] = one_hot(back_index(c)[:, 0:1] // BLK, crows)

        def scatter_some(s, carry):
            lower = cell[:, pl.ds(pl.multiple_of(s * BLK, BLK), BLK)] & 31
            hot_spread[s] = jnp.concatenate(
                [jnp.where(lower == l, 1.0, 0.0) for l in range(32)], axis=0
            ).astype(jnp.bfloat16)
            return carry

        lax.fori_loop(0, slots, scatter_some, 0, unroll=4)
        wait_items(first_items)

        def set_ghost(t, s, value):
            if s < 2:
                field[t, 0 if s == 0 else cx + 1] = value
            else:
                yrecv[t, s - 2] = value

        for s in range(4):
            set_ghost(0, s, layer(first_in, s, 0))
            low, high = ends[s]
            set_ghost(1, s, (
                layer(first_in, s, 1) + layer(first_in, s, 2) * layer(first_out, s, 0)
                + at_ends(
                    column(first_in, s, end_row) * column(pre_in, low, 0),
                    column(first_in, s, end_row + zblocks) * column(pre_in, high, 0),
                )
            ))
        for i in range(cx):
            field[1, i + 1] = smoother_row(0, i)
        residual_inside(1)
        for i in range(cx):
            resid[i] = residual_row(1, i)
        table = jnp.concatenate(
            [resid[:, :, z * BLK:(z + 1) * BLK].reshape(cells, BLK) for z in range(zblocks)],
            axis=0,
        )
        fine_two[...] = split_two(table)

        picked = pick_hot(cell_index, hot_slot, fine_two[...])
        lanes = lax.broadcasted_iota(jnp.int32, (8, BLK), 1)
        for s in range(slots):
            live = lanes + s * BLK < counts[...]
            values = jnp.where(live, picked[8 * s:8 * s + 8], 0.0)
            for d in range(8):
                sent[d, s:s + 1, :] = values[d:d + 1]
        start_eight(slot_plan)

        step = 9 if kr % 9 == 0 else 1

        def restrict_some(c, acc):
            index = rcol[pl.ds(c * step, step)].reshape(step * crows, BLK)
            block = index[:, 0:1] // BLK
            base = jnp.where(block < fine_rows, fine_place(block), -1)
            got = pick(index, base, fine_two[...]).reshape(step, crows, BLK)
            return acc + jnp.sum(got * rval[pl.ds(c * step, step)], axis=0)

        rc = lax.fori_loop(
            0, kr // step, restrict_some, jnp.zeros((crows, BLK), jnp.float32)
        )
        far_index = rcol[:, 0:rim_rows, :].reshape(kr * rim_rows, BLK)
        hot_far = one_hot(far_index[:, 0:1] // BLK - fine_rows, 8 * slots)
        own_index = ccol[...].reshape(ka * crows, BLK)
        hot_own = one_hot(own_index[:, 0:1] // BLK, crows)
        rim_index = ccol[:, 0:rim_rows, :].reshape(ka * rim_rows, BLK)
        hot_rim = one_hot(rim_index[:, 0:1] // BLK - crows, 8 * rim_rows)
        wait_eight(slot_plan)
        received_two = split_two(received[...].reshape(8 * slots, BLK))
        got = pick_hot(far_index, hot_far, received_two)
        more = jnp.sum(
            got.reshape(kr, rim_rows, BLK) * rval[:, 0:rim_rows, :], axis=0
        )
        rc = jnp.concatenate([rc[:rim_rows] + more, rc[rim_rows:]], axis=0)

        def coarse_apply(t, vector, diagonal, values):
            coarse[t] = vector
            start_eight(rim_plan(t))
            if t > 0:
                start_items(edge_items(t - 1))
            got = pick_hot(own_index, hot_own, split_two(vector))
            own = diagonal[...] * vector + jnp.sum(
                got.reshape(ka, crows, BLK) * values[...], axis=0
            )
            wait_eight(rim_plan(t))
            got = pick_hot(
                rim_index, hot_rim, split_two(rim[t].reshape(8 * rim_rows, BLK))
            )
            more = jnp.sum(
                got.reshape(ka, rim_rows, BLK) * values[:, 0:rim_rows, :], axis=0
            )
            return jnp.concatenate([own[:rim_rows] + more, own[rim_rows:]], axis=0)

        xc1 = coarse_apply(0, rc, mdiag, mval)
        rc2 = rc - coarse_apply(1, xc1, cdiag, cval)
        xc2 = xc1 + coarse_apply(2, rc2, mdiag, mval)
        coarse_two = split_two(xc2)

        for c in range(slots // group):
            parts = [(c * group + g) * BLK for g in range(group)]
            got = pick_hot(
                back_index(c), hot_back[c * batch:(c + 1) * batch], coarse_two
            )
            for g, p in enumerate(parts):
                mine = got[g * ki * 8:(g + 1) * ki * 8].reshape(ki, 8, BLK)
                values = jnp.sum(mine * rrval[:, :, p:p + BLK], axis=0)
                for d in range(8):
                    back[d, c * group + g:c * group + g + 1, :] = values[d:d + 1]
        start_eight(back_plan)
        start_items(edge_items(2))

        for z in range(zblocks):
            p = z * BLK
            index = irow[:, :, :, p:p + BLK].reshape(ki * cells, BLK)
            got = pick(index, index[:, 0:1] // BLK, coarse_two)
            got = got.reshape(ki, cx, cy, BLK) * ival[:, :, :, p:p + BLK]
            field[2, 1:cx + 1, :, p:p + BLK] = (
                field[1, 1:cx + 1, :, p:p + BLK] + jnp.sum(got, axis=0)
            )
        wait_eight(back_plan)

        fold_rows = lax.broadcasted_iota(jnp.int32, (32, BLK), 0)
        fold_lanes = lax.broadcasted_iota(jnp.int32, (32, BLK), 1)
        fold_index = (fold_lanes % 16) * 8 + fold_rows % 8
        fold_left = jnp.logical_and(fold_lanes // 32 == fold_rows // 8, fold_lanes % 32 < 16)
        fold_right = jnp.logical_and(fold_lanes // 32 == fold_rows // 8, fold_lanes % 32 >= 16)

        def spread_some(s, carry):
            p = pl.multiple_of(s * BLK, BLK)
            values = jnp.concatenate(
                [returned[d, pl.ds(s, 1), :] for d in range(8)], axis=0
            )
            values = jnp.where(lanes + p < counts[...], values, 0.0)
            upper = (cell[:, pl.ds(p, BLK)] & (BLK - 1)) // 32
            coarse_part = jnp.concatenate(
                [jnp.where(upper == h, values, 0.0) for h in range(4)], axis=0
            )
            high = coarse_part.astype(jnp.bfloat16)
            low = (coarse_part - high.astype(jnp.float32)).astype(jnp.bfloat16)
            out = lax.dot_general(
                jnp.concatenate([high, low], axis=0), hot_spread[s],
                (((1,), (1,)), ((), ())), preferred_element_type=jnp.float32,
            )
            out = out[:32] + out[32:]
            left = jnp.take_along_axis(
                out[:, :BLK], fold_index, axis=1, mode="promise_in_bounds"
            )
            right = jnp.take_along_axis(
                out[:, BLK:], fold_index, axis=1, mode="promise_in_bounds"
            )
            out = jnp.where(fold_left, left, jnp.where(fold_right, right, 0.0))
            out = jnp.sum(out.reshape(4, 8, BLK), axis=0)
            spread[pl.ds(pl.multiple_of(s * 8, 8), 8)] = out
            return carry

        lax.fori_loop(0, slots, spread_some, 0, unroll=32)
        both = jnp.dot(
            choose[...], split_two(spread[...]), preferred_element_type=jnp.float32
        )
        added = both[:, :BLK] + both[:, BLK:]
        for z in range(zblocks):
            p = z * BLK
            field[2, 1:cx + 1, :, p:p + BLK] = (
                field[2, 1:cx + 1, :, p:p + BLK]
                + added[z * cells:(z + 1) * cells].reshape(cx, cy, BLK)
            )
        for i in range(cx):
            put_edges(last_out, 0, i, field[2, i + 1])
        start_items(early_items)
        residual_inside(2)
        for i in range(cx):
            field[3, i + 1] = partial[i]
        smoother_inside(3, 2)
        for i in range(cx):
            put_edges(last_out, 1, i, field[3, i + 1])
            put_edges(last_out, 2, i, partial[i])
        for c in range(4):
            i, j, di, dj = corner_cell(c)
            put_column(tip_out, c, 0, field[2, i + 1][j:j + 1])
            put_column(tip_out, c, zblocks, field[2, i + 1][j + dj:j + dj + 1])
            put_column(tip_out, c, 2 * zblocks, field[2, i + 1 + di][j:j + 1])
            put_column(tip_out, c, 3 * zblocks, field[3, i + 1][j:j + 1])
        start_items(last_items)
        for t in range(3):
            wait_items(edge_items(t))
        wait_items(early_items)
        wait_items(last_items)

        beyond = [layer(last_in, s, 0) for s in range(4)]
        for s in range(4):
            set_ghost(2, s, beyond[s])
        corner_resid = []
        for c in range(4):
            i, j, _, _ = corner_cell(c)
            sx, sy = (0 if i == 0 else 1), (2 if j == 0 else 3)
            value = (
                column(tip_in, c, 3 * zblocks) + beyond[sx][j:j + 1] + beyond[sy][i:i + 1]
            )
            corner_resid.append(jnp.where(exists[CORNERS[c]], value, 0.0))

        for s in range(4):
            low, high = ends[s]
            low_face, high_face = along[s]
            place = 0 if s % 2 == 0 else cy - 1
            low_side, high_side = (2, 3) if s < 2 else (0, 1)
            change = layer(last_out, s, 0) + at_ends(
                column(tip_in, low, 0), column(tip_in, high, 0)
            )
            beyond_resid = jnp.where(
                side_exists[s], layer(last_in, s, 1) + change, 0.0
            )
            set_ghost(3, s, beyond_resid)
            own_resid = layer(last_out, s, 1) + beyond[s] + at_ends(
                beyond[low_side][place:place + 1], beyond[high_side][place:place + 1]
            )
            wide = (cy, nz)
            before = jnp.where(
                first_row, jnp.broadcast_to(corner_resid[low], wide), pltpu.roll(change, 1, 0)
            )
            after = jnp.where(
                last_row, jnp.broadcast_to(corner_resid[high], wide),
                pltpu.roll(change, cy - 1, 0),
            )
            column_low = zblocks if s >= 2 else 2 * zblocks
            second = at_ends(
                column(tip_in, low, column_low), column(tip_in, high, column_low)
            )
            set_ghost(4, s, (
                layer(last_in, s, 2)
                + edges_in[s, 0] * change
                + edges_in[s, low_face] * before
                + edges_in[s, high_face] * after
                + edges_in[s, facing[s]] * own_resid
                + edges_in[s, away[s]] * second
                + edges_in[s, 5] * jnp.where(lane_ids == 0, 0.0, pltpu.roll(change, 1, 1))
                + edges_in[s, 6] * jnp.where(lane_ids == nz - 1, 0.0, pltpu.roll(change, nz - 1, 1))
            ))
        for i in range(cx):
            partial[i] = field[3, i + 1]
        for i in range(cx):
            field[3, i + 1] = residual_row(2, i)
        smoother_inside(3, 2)
        for i in range(cx):
            value = smoother_row(3, i)
            field[4, i + 1] = value
            sol_ref[i] = value
        residual_inside(4)
        for i in range(cx):
            res_ref[i] = residual_row(4, i)

        finish_items(first_items)
        finish_items(early_items)
        finish_items(last_items)
        for t in range(3):
            finish_items(edge_items(t))
        for plan in (slot_plan, back_plan, rim_plan(0), rim_plan(1), rim_plan(2)):
            for d in range(8):
                @pl.when(exists[d])
                def _():
                    eight_copy(*plan, d).wait_send()

    f32, i32, bf16 = jnp.float32, jnp.int32, jnp.bfloat16
    vm = pltpu.VMEM
    dma = pltpu.SemaphoreType.DMA
    scratch = [
        vm((ki * 8 * slots, crows), bf16), vm((slots, 256, BLK), bf16),
        pltpu.SMEM((1, 1, 8), i32), vm((8, BLK), i32),
        vm((5, cx + 2, cy, nz), f32), vm((5, 2, cx, nz), f32),
        vm((cx, cy, nz), f32), vm((cx, cy, nz), f32), vm((6, cx, cy, nz), f32),
        vm((4, 7, 8, nz), f32),
        vm((8, cap), i32), vm((kr, crows, BLK), i32), vm((kr, crows, BLK), f32),
        vm((ka, crows, BLK), i32), vm((crows, BLK), f32), vm((ka, crows, BLK), f32),
        vm((crows, BLK), f32), vm((ka, crows, BLK), f32),
        vm((ki, 8, cap), i32), vm((ki, 8, cap), f32),
        vm((ki, cx, cy, nz), i32), vm((ki, cx, cy, nz), f32),
        vm((cx, cy, nz), f32), vm((fine_rows, 2 * BLK), bf16),
        vm((fine_rows, 8 * slots), bf16),
        vm((8, slots, BLK), f32), vm((8, slots, BLK), f32),
        vm((8, slots, BLK), f32), vm((8, slots, BLK), f32),
        vm((3, crows, BLK), f32), vm((3, 8, rim_rows, BLK), f32),
        vm((8 * slots, BLK), f32), vm((cx, cy, nz), f32),
        vm((4, (3 * 8 + 2) * zblocks, BLK), f32), vm((4, (3 * 8 + 2) * zblocks, BLK), f32),
        vm((4, zblocks, BLK), f32), vm((4, zblocks, BLK), f32),
        vm((4, 3 * 8 * zblocks, BLK), f32), vm((4, 3 * 8 * zblocks, BLK), f32),
        vm((4, 4 * zblocks, BLK), f32), vm((4, 4 * zblocks, BLK), f32),
        vm((4, 7, 8, nz), f32),
        dma((25,)), dma((4,)), dma((4,)), dma((4,)), dma((4,)), dma((2, 4)), dma((2, 4)),
        dma((4,)), dma((4,)), dma((3, 4)), dma((3, 4)),
        dma((8,)), dma((8,)), dma((8,)), dma((8,)),
        dma((3, 8)), dma((3, 8)),
    ]
    whole = pl.BlockSpec(memory_space=pltpu.VMEM)
    in_hbm = pl.BlockSpec(memory_space=pltpu.HBM)
    return pl.pallas_call(
        kernel,
        out_shape=(
            jax.ShapeDtypeStruct((cx, cy, nz), f32),
            jax.ShapeDtypeStruct((cx, cy, nz), f32),
        ),
        in_specs=[in_hbm] * 17,
        out_specs=(whole, whole),
        scratch_shapes=scratch,
        compiler_params=pltpu.CompilerParams(
            collective_id=0, has_side_effects=True, vmem_limit_bytes=40 * 1024 * 1024
        ),
        name="vcycle",
    )


def write_out(first, second):
    def kernel(first_ref, second_ref, first_out, second_out, sem):
        copies = [
            pltpu.make_async_copy(first_ref, first_out, sem.at[0]),
            pltpu.make_async_copy(second_ref, second_out, sem.at[1]),
        ]
        for copy in copies:
            copy.start()
        for copy in copies:
            copy.wait()

    return pl.pallas_call(
        kernel,
        out_shape=(
            jax.ShapeDtypeStruct(first.shape, first.dtype),
            jax.ShapeDtypeStruct(second.shape, second.dtype),
        ),
        in_specs=[pl.BlockSpec(memory_space=pltpu.VMEM)] * 2,
        out_specs=(pl.BlockSpec(memory_space=pltpu.HBM),) * 2,
        scratch_shapes=[pltpu.SemaphoreType.DMA((2,))],
        compiler_params=pltpu.CompilerParams(vmem_limit_bytes=4 * 1024 * 1024),
        name="write_out",
    )(first, second)


def body(
    rhs, diag, smoother_center, smoother_faces, send_count, send_cell, restrict_col,
    restrict_vals, coarse_col, coarse_diag, coarse_vals, csmooth_diag, csmooth_vals,
    remote_row, remote_vals, interp_row, interp_vals,
):
    def rows(array):
        return array.reshape(array.shape[0], -1, BLK)

    cap = send_cell.shape[-1]
    ki = remote_row.shape[0]
    def in_hbm(array):
        return pltpu.with_memory_space_constraint(array, pltpu.HBM)

    operands = (
        rhs, diag, smoother_center, smoother_faces,
        send_count,
        send_cell.reshape(8, cap), rows(restrict_col), rows(restrict_vals),
        rows(coarse_col), coarse_diag.reshape(-1, BLK), rows(coarse_vals),
        csmooth_diag.reshape(-1, BLK), rows(csmooth_vals),
        remote_row.reshape(ki, 8, cap), remote_vals.reshape(ki, 8, cap),
        interp_row, interp_vals,
    )
    shapes = {
        "rhs": rhs.shape, "send_cell": (8, cap), "restrict_col": operands[6].shape,
        "coarse_col": operands[8].shape, "interp_row": interp_row.shape,
    }
    sizes = (lax.axis_size("gx"), lax.axis_size("gy"))
    operands = [in_hbm(x) for x in operands]
    return write_out(*make_kernel(sizes, shapes)(*operands))


def solution(mesh):
    fine = P("gx", "gy", None)
    listed = P(None, "gx", "gy", None)
    placed = (
        fine, fine, fine, listed, fine, P("gx", "gy", None, None), listed, listed,
        listed, fine, listed, fine, listed,
        P(None, "gx", "gy", None, None), P(None, "gx", "gy", None, None),
        listed, listed,
    )
    return jax.shard_map(
        body, mesh=mesh, in_specs=placed, out_specs=(fine, fine), check_vma=False
    )
```

time: 38.5 us -> 36.3 us (0.943)
  local copies, waits for them, and re-layouts: 2.03 us -> 0 us
    unnamed x4 -> x0, local copies, waits for them, and re-layouts: 1.96 us -> none
    pallas_call x1 -> x2, Pallas kernels: 35.7 us -> 35.5 us  [the longest x1 34.8 us: body(): return write_out(*make_kernel(sizes, shapes)(*operands))]
where the time goes in v2:
time: 36.3 us; the launch traced here: 36.2 us
  Pallas kernels  35.5 us (98%)
  between operations  0.65 us (2%)
    pallas_call x1, Pallas kernels, body(): return write_out(*make_kernel(sizes, shapes)(*operands))  34.8 us

profile of v2, /device:TPU:0, one launch (start us, length us, event | category | flops | bytes accessed | tf_op | source)
XLA Modules:
  0.0 36.2 jit_solution(7810629007871494368)
XLA Ops:
  0.6 34.8 %vcycle.1 = (f32[8,8,512]{2,1,0:T(8,128)S(1)}, f32[8,8,512]{2,1,0:T(8,128)S(1)}) custom-call(f32[8,8,512]{2,1,0:T(8,128)} %rhs_h.1, f32[8,8,512]{2,1,0:T(8,128)} %diag_h.1, f32[8,8,512]{2,1,0:T(8,128)} %center_h.1, f32[6,8,8,512]{3,2,1,0:T(8,128)} %faces_h.1, s32[1,1,8]{2,1,0:T(1,128)} %count_h.1, s32[8,4096]{1,0:T(8,128)} %bitcast.17, ...), custom_call_target="tpu_custom_call" | custom-call | tf_op jit(solution)/shard_map/vcycle/pallas_call | solution.py:781
  35.5 0.7 %write_out.1 = (f32[8,8,512]{2,1,0:T(8,128)}, f32[8,8,512]{2,1,0:T(8,128)}) custom-call(f32[8,8,512]{2,1,0:T(8,128)S(1)} %get-tuple-element.4.first_ref, f32[8,8,512]{2,1,0:T(8,128)S(1)} %get-tuple-element.5.second_ref), custom_call_target="tpu_custom_call" | custom-call | tf_op jit(solution)/shard_map/write_out/pallas_call | solution.py:739

commit v3 on v2

--- a/solution.py
+++ b/solution.py
@@ -53,11 +53,11 @@
         rhs_h, diag_h, center_h, faces_h, count_h, cell_h, rcol_h, rval_h, ccol_h,
         cdiag_h, cval_h, mdiag_h, mval_h, rrow_h, rrval_h, irow_h, ival_h,
         sol_ref, res_ref,
-        hot_back, hot_spread, count, counts, field, yrecv, diag, center, faces, edges, cell, rcol, rval, ccol, cdiag, cval,
+        hot_back, hot_spread, turned, count, counts, field, yrecv, diag, center, faces, edges, cell, rcol, rval, ccol, cdiag, cval,
         mdiag, mval, rrow, rrval, irow, ival, resid, fine_two, choose, sent, received,
         back, returned, coarse, rim, spread, partial,
         first_out, first_in, pre_out, pre_in, last_out, last_in, tip_out, tip_in, edges_in,
-        in_sem, first_send, first_recv, pre_send, pre_recv, last_send, last_recv,
+        ends_out, ends_in, in_sem, first_send, first_recv, pre_send, pre_recv, last_send, last_recv,
         tip_send, tip_recv, edges_send, edges_recv,
         slot_send, slot_recv, back_send, back_recv, rim_send, rim_recv,
     ):
@@ -68,10 +68,12 @@
             (rhs_h, field.at[0, pl.ds(1, cx)]), (center_h, center), (faces_h, faces),
             (center_h.at[0], edges.at[0, 0]), (center_h.at[cx - 1], edges.at[1, 0]),
             (center_h.at[:, 0, :], edges.at[2, 0]), (center_h.at[:, cy - 1, :], edges.at[3, 0]),
-            (faces_h.at[:, 0], edges.at[0, pl.ds(1, 6)]),
-            (faces_h.at[:, cx - 1], edges.at[1, pl.ds(1, 6)]),
-            (faces_h.at[:, :, 0, :], edges.at[2, pl.ds(1, 6)]),
-            (faces_h.at[:, :, cy - 1, :], edges.at[3, pl.ds(1, 6)]),
+            (faces_h.at[pl.ds(2, 4), 0], edges.at[0, pl.ds(1, 4)]),
+            (faces_h.at[pl.ds(2, 4), cx - 1], edges.at[1, pl.ds(1, 4)]),
+            (faces_h.at[pl.ds(0, 2), :, 0, :], edges.at[2, pl.ds(1, 2)]),
+            (faces_h.at[pl.ds(4, 2), :, 0, :], edges.at[2, pl.ds(3, 2)]),
+            (faces_h.at[pl.ds(0, 2), :, cy - 1, :], edges.at[3, pl.ds(1, 2)]),
+            (faces_h.at[pl.ds(4, 2), :, cy - 1, :], edges.at[3, pl.ds(3, 2)]),
             (diag_h, diag), (cell_h, cell), (count_h, count), (rcol_h, rcol), (rval_h, rval),
             (ccol_h, ccol), (mdiag_h, mdiag), (mval_h, mval), (cdiag_h, cdiag),
             (cval_h, cval), (rrow_h, rrow), (rrval_h, rrval), (irow_h, irow),
@@ -165,12 +167,23 @@
         )
 
         def edge_items(t):
-            low, size = ((0, 3), (3, 2), (5, 2))[t]
-            return side_items(
+            if t == 3:
+                return side_items(
+                    lambda s: ends_out.at[s], lambda s: ends_in.at[s],
+                    lambda s: edges_send.at[t, s], lambda s: edges_recv.at[t, s],
+                )
+            low, size = ((0, 2), (2, 2), (4, 1))[t]
+            items = side_items(
                 lambda s: edges.at[s, pl.ds(low, size)],
                 lambda s: edges_in.at[s, pl.ds(low, size)],
                 lambda s: edges_send.at[t, s], lambda s: edges_recv.at[t, s],
-            )
+            )[0:2]
+            if t == 0:
+                items = items + side_items(
+                    lambda s: edges.at[s], lambda s: edges_in.at[s],
+                    lambda s: edges_send.at[t, s], lambda s: edges_recv.at[t, s],
+                )[2:4]
+            return items
 
         def start_items(items):
             for cond, copy, _ in items:
@@ -319,9 +332,6 @@
             dx, dy = OFFSETS[CORNERS[c]]
             return (0 if dx < 0 else cx - 1), (0 if dy < 0 else cy - 1), -dx, -dy
 
-        away = [1 + s for s in range(4)]
-        facing = [1 + (s ^ 1) for s in range(4)]
-        along = [(3, 4), (3, 4), (1, 2), (1, 2)]
         ends = [(0, 1), (2, 3), (0, 2), (1, 3)]
         first_row, last_row = row_ids == 0, row_ids == cy - 1
 
@@ -334,6 +344,8 @@
 
         for load in loads[0:3]:
             load.wait()
+        for load in loads[3:]:
+            load.start()
         smoother_inside(0, None)
         for i in range(cx):
             put_edges(first_out, 0, i, field[0, i + 1])
@@ -364,14 +376,13 @@
                 first_out[s, row_high:row_high + 1, :] = at_high
         pl.semaphore_wait(barrier, total)
         start_items(first_items)
-        for load in loads[3:]:
-            load.start()
         for s in range(4):
             @pl.when(jnp.logical_not(side_exists[s]))
             def _():
                 first_in[s] = jnp.zeros(first_in.shape[1:], jnp.float32)
                 last_in[s] = jnp.zeros(last_in.shape[1:], jnp.float32)
                 edges_in[s] = jnp.zeros(edges_in.shape[1:], jnp.float32)
+                ends_in[s] = jnp.zeros(ends_in.shape[1:], jnp.float32)
         for c in range(4):
             @pl.when(jnp.logical_not(exists[CORNERS[c]]))
             def _():
@@ -385,7 +396,7 @@
                 for t in range(3):
                     rim[t, d] = jnp.zeros((rim_rows, BLK), jnp.float32)
 
-        edge_loads, loads = loads[3:11], loads[10:]
+        edge_loads, loads = loads[3:13], loads[12:]
         for load in loads[1:4]:
             load.wait()
         slot_rows = lax.broadcasted_iota(jnp.int32, (8, BLK), 0)
@@ -419,10 +430,28 @@
         for c in range(slots // group):
             hot_back[c * batch:(c + 1) * batch] = one_hot(back_index(c)[:, 0:1] // BLK, crows)
 
+        for s in range(4):
+            place = (0 if s % 2 == 0 else (cx if s < 2 else cy) - 1)
+            for z in range(zblocks):
+                p = z * BLK
+                if s < 2:
+                    at_low = faces[s ^ 1, place, 0:1, p:p + BLK]
+                    at_high = faces[s ^ 1, place, cy - 1:cy, p:p + BLK]
+                else:
+                    at_low = faces[s ^ 1, 0, place:place + 1, p:p + BLK]
+                    at_high = faces[s ^ 1, cx - 1, place:place + 1, p:p + BLK]
+                ends_out[s, z:z + 1, :] = at_low
+                ends_out[s, zblocks + z:zblocks + z + 1, :] = at_high
+        low_ids = lax.broadcasted_iota(jnp.int32, (32, BLK), 0)
+
         def scatter_some(s, carry):
             lower = cell[:, pl.ds(pl.multiple_of(s * BLK, BLK), BLK)] & 31
             hot_spread[s] = jnp.concatenate(
-                [jnp.where(lower == l, 1.0, 0.0) for l in range(32)], axis=0
+                [
+                    jnp.where(jnp.broadcast_to(lower[d:d + 1], (32, BLK)) == low_ids, 1.0, 0.0)
+                    for d in range(8)
+                ],
+                axis=0,
             ).astype(jnp.bfloat16)
             return carry
 
@@ -458,11 +487,11 @@
 
         picked = pick_hot(cell_index, hot_slot, fine_two[...])
         lanes = lax.broadcasted_iota(jnp.int32, (8, BLK), 1)
-        for s in range(slots):
-            live = lanes + s * BLK < counts[...]
-            values = jnp.where(live, picked[8 * s:8 * s + 8], 0.0)
-            for d in range(8):
-                sent[d, s:s + 1, :] = values[d:d + 1]
+        slot_ids = lax.broadcasted_iota(jnp.int32, (slots, 8, BLK), 0) * BLK + lanes[None]
+        values = jnp.where(
+            slot_ids < counts[...][None], picked.reshape(slots, 8, BLK), 0.0
+        )
+        sent[...] = jnp.swapaxes(values, 0, 1)
         start_eight(slot_plan)
 
         step = 9 if kr % 9 == 0 else 1
@@ -494,8 +523,9 @@
         def coarse_apply(t, vector, diagonal, values):
             coarse[t] = vector
             start_eight(rim_plan(t))
-            if t > 0:
-                start_items(edge_items(t - 1))
+            start_items(edge_items(t))
+            if t == 2:
+                start_items(edge_items(3))
             got = pick_hot(own_index, hot_own, split_two(vector))
             own = diagonal[...] * vector + jnp.sum(
                 got.reshape(ka, crows, BLK) * values[...], axis=0
@@ -519,13 +549,12 @@
             got = pick_hot(
                 back_index(c), hot_back[c * batch:(c + 1) * batch], coarse_two
             )
+            values = []
             for g, p in enumerate(parts):
                 mine = got[g * ki * 8:(g + 1) * ki * 8].reshape(ki, 8, BLK)
-                values = jnp.sum(mine * rrval[:, :, p:p + BLK], axis=0)
-                for d in range(8):
-                    back[d, c * group + g:c * group + g + 1, :] = values[d:d + 1]
+                values.append(jnp.sum(mine * rrval[:, :, p:p + BLK], axis=0))
+            back[:, c * group:(c + 1) * group, :] = jnp.swapaxes(jnp.stack(values), 0, 1)
         start_eight(back_plan)
-        start_items(edge_items(2))
 
         for z in range(zblocks):
             p = z * BLK
@@ -537,40 +566,33 @@
             )
         wait_eight(back_plan)
 
-        fold_rows = lax.broadcasted_iota(jnp.int32, (32, BLK), 0)
-        fold_lanes = lax.broadcasted_iota(jnp.int32, (32, BLK), 1)
-        fold_index = (fold_lanes % 16) * 8 + fold_rows % 8
-        fold_left = jnp.logical_and(fold_lanes // 32 == fold_rows // 8, fold_lanes % 32 < 16)
-        fold_right = jnp.logical_and(fold_lanes // 32 == fold_rows // 8, fold_lanes % 32 >= 16)
+        in_place = lanes // 32 == slot_rows % 4
 
         def spread_some(s, carry):
             p = pl.multiple_of(s * BLK, BLK)
-            values = jnp.concatenate(
-                [returned[d, pl.ds(s, 1), :] for d in range(8)], axis=0
-            )
-            values = jnp.where(lanes + p < counts[...], values, 0.0)
-            upper = (cell[:, pl.ds(p, BLK)] & (BLK - 1)) // 32
-            coarse_part = jnp.concatenate(
-                [jnp.where(upper == h, values, 0.0) for h in range(4)], axis=0
-            )
-            high = coarse_part.astype(jnp.bfloat16)
-            low = (coarse_part - high.astype(jnp.float32)).astype(jnp.bfloat16)
-            out = lax.dot_general(
-                jnp.concatenate([high, low], axis=0), hot_spread[s],
-                (((1,), (1,)), ((), ())), preferred_element_type=jnp.float32,
-            )
-            out = out[:32] + out[32:]
-            left = jnp.take_along_axis(
-                out[:, :BLK], fold_index, axis=1, mode="promise_in_bounds"
-            )
-            right = jnp.take_along_axis(
-                out[:, BLK:], fold_index, axis=1, mode="promise_in_bounds"
-            )
-            out = jnp.where(fold_left, left, jnp.where(fold_right, right, 0.0))
-            out = jnp.sum(out.reshape(4, 8, BLK), axis=0)
+            values = jnp.where(lanes + p < counts[...], turned[s], 0.0)
+            high = values.astype(jnp.bfloat16).astype(jnp.float32)
+            low = values - high
+            turn = ((cell[:, pl.ds(p, BLK)] & (BLK - 1)) // 32 - slot_rows) & 3
+            left_side = jnp.concatenate(
+                [jnp.where(turn == h, part, 0.0) for part in (high, low) for h in range(4)],
+                axis=0,
+            ).astype(jnp.bfloat16)
+            both = lax.dot_general(
+                left_side, hot_spread[s], (((1,), (1,)), ((), ())),
+                preferred_element_type=jnp.float32,
+            )
+            both = both[:32] + both[32:]
+            out = jnp.zeros((8, BLK), jnp.float32)
+            for h in range(4):
+                near = both[8 * h:8 * h + 8]
+                near = jnp.where(slot_rows < 4, near[:, :BLK], near[:, BLK:])
+                near = jnp.where(in_place, near, 0.0)
+                out = out + (pltpu.roll(near, 32 * h, 1) if h else near)
             spread[pl.ds(pl.multiple_of(s * 8, 8), 8)] = out
             return carry
 
+        turned[...] = jnp.swapaxes(returned[...], 0, 1)
         lax.fori_loop(0, slots, spread_some, 0, unroll=32)
         both = jnp.dot(
             choose[...], split_two(spread[...]), preferred_element_type=jnp.float32
@@ -599,7 +621,7 @@
             put_column(tip_out, c, 2 * zblocks, field[2, i + 1 + di][j:j + 1])
             put_column(tip_out, c, 3 * zblocks, field[3, i + 1][j:j + 1])
         start_items(last_items)
-        for t in range(3):
+        for t in range(4):
             wait_items(edge_items(t))
         wait_items(early_items)
         wait_items(last_items)
@@ -618,7 +640,6 @@
 
         for s in range(4):
             low, high = ends[s]
-            low_face, high_face = along[s]
             place = 0 if s % 2 == 0 else cy - 1
             low_side, high_side = (2, 3) if s < 2 else (0, 1)
             change = layer(last_out, s, 0) + at_ends(
@@ -641,17 +662,18 @@
             )
             column_low = zblocks if s >= 2 else 2 * zblocks
             second = at_ends(
-                column(tip_in, low, column_low), column(tip_in, high, column_low)
+                column(ends_in, s, 0) * column(tip_in, low, column_low),
+                column(ends_in, s, zblocks) * column(tip_in, high, column_low),
             )
             set_ghost(4, s, (
                 layer(last_in, s, 2)
                 + edges_in[s, 0] * change
-                + edges_in[s, low_face] * before
-                + edges_in[s, high_face] * after
-                + edges_in[s, facing[s]] * own_resid
-                + edges_in[s, away[s]] * second
-                + edges_in[s, 5] * jnp.where(lane_ids == 0, 0.0, pltpu.roll(change, 1, 1))
-                + edges_in[s, 6] * jnp.where(lane_ids == nz - 1, 0.0, pltpu.roll(change, nz - 1, 1))
+                + edges_in[s, 1] * before
+                + edges_in[s, 2] * after
+                + layer(first_in, s, 2) * own_resid
+                + second
+                + edges_in[s, 3] * jnp.where(lane_ids == 0, 0.0, pltpu.roll(change, 1, 1))
+                + edges_in[s, 4] * jnp.where(lane_ids == nz - 1, 0.0, pltpu.roll(change, nz - 1, 1))
             ))
         for i in range(cx):
             partial[i] = field[3, i + 1]
@@ -669,7 +691,7 @@
         finish_items(first_items)
         finish_items(early_items)
         finish_items(last_items)
-        for t in range(3):
+        for t in range(4):
             finish_items(edge_items(t))
         for plan in (slot_plan, back_plan, rim_plan(0), rim_plan(1), rim_plan(2)):
             for d in range(8):
@@ -681,11 +703,11 @@
     vm = pltpu.VMEM
     dma = pltpu.SemaphoreType.DMA
     scratch = [
-        vm((ki * 8 * slots, crows), bf16), vm((slots, 256, BLK), bf16),
+        vm((ki * 8 * slots, crows), bf16), vm((slots, 256, BLK), bf16), vm((slots, 8, BLK), f32),
         pltpu.SMEM((1, 1, 8), i32), vm((8, BLK), i32),
         vm((5, cx + 2, cy, nz), f32), vm((5, 2, cx, nz), f32),
         vm((cx, cy, nz), f32), vm((cx, cy, nz), f32), vm((6, cx, cy, nz), f32),
-        vm((4, 7, 8, nz), f32),
+        vm((4, 5, 8, nz), f32),
         vm((8, cap), i32), vm((kr, crows, BLK), i32), vm((kr, crows, BLK), f32),
         vm((ka, crows, BLK), i32), vm((crows, BLK), f32), vm((ka, crows, BLK), f32),
         vm((crows, BLK), f32), vm((ka, crows, BLK), f32),
@@ -701,9 +723,10 @@
         vm((4, zblocks, BLK), f32), vm((4, zblocks, BLK), f32),
         vm((4, 3 * 8 * zblocks, BLK), f32), vm((4, 3 * 8 * zblocks, BLK), f32),
         vm((4, 4 * zblocks, BLK), f32), vm((4, 4 * zblocks, BLK), f32),
-        vm((4, 7, 8, nz), f32),
-        dma((25,)), dma((4,)), dma((4,)), dma((4,)), dma((4,)), dma((2, 4)), dma((2, 4)),
-        dma((4,)), dma((4,)), dma((3, 4)), dma((3, 4)),
+        vm((4, 5, 8, nz), f32),
+        vm((4, 2 * zblocks, BLK), f32), vm((4, 2 * zblocks, BLK), f32),
+        dma((27,)), dma((4,)), dma((4,)), dma((4,)), dma((4,)), dma((2, 4)), dma((2, 4)),
+        dma((4,)), dma((4,)), dma((4, 4)), dma((4, 4)),
         dma((8,)), dma((8,)), dma((8,)), dma((8,)),
         dma((3, 8)), dma((3, 8)),
     ]

time: 36.3 us -> 35.9 us (0.989)
  Pallas kernels: 35.5 us -> 35.1 us
    pallas_call x1, Pallas kernels: 34.8 us -> 34.4 us  [body(): return write_out(*make_kernel(sizes, shapes)(*operands))]
where the time goes in v3:
time: 35.9 us; the launch traced here: 35.8 us
  Pallas kernels  35.1 us (98%)
  between operations  0.65 us (2%)
    pallas_call x1, Pallas kernels, body(): return write_out(*make_kernel(sizes, shapes)(*operands))  34.4 us

profile of v3, /device:TPU:0, one launch (start us, length us, event | category | flops | bytes accessed | tf_op | source)
XLA Modules:
  0.0 35.8 jit_solution(406825703068867989)
XLA Ops:
  0.6 34.4 %vcycle.1 = (f32[8,8,512]{2,1,0:T(8,128)S(1)}, f32[8,8,512]{2,1,0:T(8,128)S(1)}) custom-call(f32[8,8,512]{2,1,0:T(8,128)} %rhs_h.1, f32[8,8,512]{2,1,0:T(8,128)} %diag_h.1, f32[8,8,512]{2,1,0:T(8,128)} %center_h.1, f32[6,8,8,512]{3,2,1,0:T(8,128)} %faces_h.1, s32[1,1,8]{2,1,0:T(1,128)} %count_h.1, s32[8,4096]{1,0:T(8,128)} %bitcast.17, ...), custom_call_target="tpu_custom_call" | custom-call | tf_op jit(solution)/shard_map/vcycle/pallas_call | solution.py:804
  35.1 0.7 %write_out.1 = (f32[8,8,512]{2,1,0:T(8,128)}, f32[8,8,512]{2,1,0:T(8,128)}) custom-call(f32[8,8,512]{2,1,0:T(8,128)S(1)} %get-tuple-element.4.first_ref, f32[8,8,512]{2,1,0:T(8,128)S(1)} %get-tuple-element.5.second_ref), custom_call_target="tpu_custom_call" | custom-call | tf_op jit(solution)/shard_map/write_out/pallas_call | solution.py:762

commit v4 on v3

--- a/solution.py
+++ b/solution.py
@@ -178,7 +178,7 @@
                 lambda s: edges_in.at[s, pl.ds(low, size)],
                 lambda s: edges_send.at[t, s], lambda s: edges_recv.at[t, s],
             )[0:2]
-            if t == 0:
+            if t == 1:
                 items = items + side_items(
                     lambda s: edges.at[s], lambda s: edges_in.at[s],
                     lambda s: edges_send.at[t, s], lambda s: edges_recv.at[t, s],
@@ -232,6 +232,12 @@
                 lambda d: coarse.at[t, pl.ds(0, rim_rows)], lambda d: rim.at[t, d],
                 lambda d: rim_send.at[t, d], lambda d: rim_recv.at[t, d],
             )
+
+        def finish_eight(plan):
+            for d in range(8):
+                @pl.when(exists[d])
+                def _():
+                    eight_copy(*plan, d).wait_send()
 
         def start_eight(plan):
             for d in (0, 2, 5, 7, 3, 4, 1, 6):
@@ -564,6 +570,10 @@
             field[2, 1:cx + 1, :, p:p + BLK] = (
                 field[1, 1:cx + 1, :, p:p + BLK] + jnp.sum(got, axis=0)
             )
+        finish_items(first_items)
+        finish_eight(slot_plan)
+        for t in range(3):
+            finish_eight(rim_plan(t))
         wait_eight(back_plan)
 
         in_place = lanes // 32 == slot_rows % 4
@@ -621,7 +631,9 @@
             put_column(tip_out, c, 2 * zblocks, field[2, i + 1 + di][j:j + 1])
             put_column(tip_out, c, 3 * zblocks, field[3, i + 1][j:j + 1])
         start_items(last_items)
+        finish_eight(back_plan)
         for t in range(4):
+            finish_items(edge_items(t))
             wait_items(edge_items(t))
         wait_items(early_items)
         wait_items(last_items)
@@ -688,16 +700,8 @@
         for i in range(cx):
             res_ref[i] = residual_row(4, i)
 
-        finish_items(first_items)
         finish_items(early_items)
         finish_items(last_items)
-        for t in range(4):
-            finish_items(edge_items(t))
-        for plan in (slot_plan, back_plan, rim_plan(0), rim_plan(1), rim_plan(2)):
-            for d in range(8):
-                @pl.when(exists[d])
-                def _():
-                    eight_copy(*plan, d).wait_send()
 
     f32, i32, bf16 = jnp.float32, jnp.int32, jnp.bfloat16
     vm = pltpu.VMEM

time: 35.9 us -> 35.9 us (level)
  no operation moved by 1% of the time
where the time goes in v4:
time: 35.9 us; the launch traced here: 35.7 us
  Pallas kernels  35.1 us (98%)
  between operations  0.65 us (2%)
    pallas_call x1, Pallas kernels, body(): return write_out(*make_kernel(sizes, shapes)(*operands))  34.4 us

profile of v4, /device:TPU:0, one launch (start us, length us, event | category | flops | bytes accessed | tf_op | source)
XLA Modules:
  0.0 35.7 jit_solution(12753885279417222959)
XLA Ops:
  0.6 34.4 %vcycle.1 = (f32[8,8,512]{2,1,0:T(8,128)S(1)}, f32[8,8,512]{2,1,0:T(8,128)S(1)}) custom-call(f32[8,8,512]{2,1,0:T(8,128)} %rhs_h.1, f32[8,8,512]{2,1,0:T(8,128)} %diag_h.1, f32[8,8,512]{2,1,0:T(8,128)} %center_h.1, f32[6,8,8,512]{3,2,1,0:T(8,128)} %faces_h.1, s32[1,1,8]{2,1,0:T(1,128)} %count_h.1, s32[8,4096]{1,0:T(8,128)} %bitcast.17, ...), custom_call_target="tpu_custom_call" | custom-call | tf_op jit(solution)/shard_map/vcycle/pallas_call | solution.py:808
  35.0 0.7 %write_out.1 = (f32[8,8,512]{2,1,0:T(8,128)}, f32[8,8,512]{2,1,0:T(8,128)}) custom-call(f32[8,8,512]{2,1,0:T(8,128)S(1)} %get-tuple-element.4.first_ref, f32[8,8,512]{2,1,0:T(8,128)S(1)} %get-tuple-element.5.second_ref), custom_call_target="tpu_custom_call" | custom-call | tf_op jit(solution)/shard_map/write_out/pallas_call | solution.py:766

commit v5 on v4

--- a/solution.py
+++ b/solution.py
@@ -113,7 +113,7 @@
                 )
             total = total + exists[d].astype(jnp.int32)
 
-        for load in loads[:3]:
+        for load in loads:
             load.start()
 
         def item(cond, step, src, there_ref, here_ref, send, there_sem, here_sem):
@@ -350,8 +350,6 @@
 
         for load in loads[0:3]:
             load.wait()
-        for load in loads[3:]:
-            load.start()
         smoother_inside(0, None)
         for i in range(cx):
             put_edges(first_out, 0, i, field[0, i + 1])

time: 35.9 us -> 35.9 us (level)
  no operation moved by 1% of the time
where the time goes in v5:
time: 35.9 us; the launch traced here: 35.7 us
  Pallas kernels  35.1 us (98%)
  between operations  0.65 us (2%)
    pallas_call x1, Pallas kernels, body(): return write_out(*make_kernel(sizes, shapes)(*operands))  34.4 us

profile of v5, /device:TPU:0, one launch (start us, length us, event | category | flops | bytes accessed | tf_op | source)
XLA Modules:
  0.0 35.7 jit_solution(4400142776782220104)
XLA Ops:
  0.6 34.4 %vcycle.1 = (f32[8,8,512]{2,1,0:T(8,128)S(1)}, f32[8,8,512]{2,1,0:T(8,128)S(1)}) custom-call(f32[8,8,512]{2,1,0:T(8,128)} %rhs_h.1, f32[8,8,512]{2,1,0:T(8,128)} %diag_h.1, f32[8,8,512]{2,1,0:T(8,128)} %center_h.1, f32[6,8,8,512]{3,2,1,0:T(8,128)} %faces_h.1, s32[1,1,8]{2,1,0:T(1,128)} %count_h.1, s32[8,4096]{1,0:T(8,128)} %bitcast.17, ...), custom_call_target="tpu_custom_call" | custom-call | tf_op jit(solution)/shard_map/vcycle/pallas_call | solution.py:806
  35.0 0.7 %write_out.1 = (f32[8,8,512]{2,1,0:T(8,128)}, f32[8,8,512]{2,1,0:T(8,128)}) custom-call(f32[8,8,512]{2,1,0:T(8,128)S(1)} %get-tuple-element.4.first_ref, f32[8,8,512]{2,1,0:T(8,128)S(1)} %get-tuple-element.5.second_ref), custom_call_target="tpu_custom_call" | custom-call | tf_op jit(solution)/shard_map/write_out/pallas_call | solution.py:764
